TPU v7x, 32 devices: a whole 2x2x4 slice. The times are simulated.
32 devices in a mesh: dp: 4 (over x, core), fsdp: 8 (over z, y).
Axes of the slice: x: 2, y: 2, z: 4, core: 2. Of those that a mesh axis runs over, the one named last changes fastest.
Arguments:
- text_in: bfloat16 [512, 64, 768], P(('dp', 'fsdp')), may hold values from -6 to 6
- text_segments: int32 [512, 64], P(('dp', 'fsdp')), may hold values from 0 to 8, never falling along the last dimension, each value on 1 to 32 neighbouring positions
- text_cotangent: bfloat16 [512, 64, 768], P(('dp', 'fsdp')), may hold values from -6 to 6
- image_in: bfloat16 [128, 50, 768], P(('dp', 'fsdp')), may hold values from -6 to 6
- ln1_gain: bfloat16 [768], P('fsdp'), may hold values from 0.25 to 1.75
- ln1_bias: bfloat16 [768], P('fsdp'), may hold values from -4 to 4
- w_qkv: bfloat16 [768, 2304], P('fsdp'), may hold values from -0.21875 to 0.21875
- q_bias: bfloat16 [768], P('fsdp'), may hold values from -4 to 4
- v_bias: bfloat16 [768], P('fsdp'), may hold values from -4 to 4
- w_out: bfloat16 [768, 768], P('fsdp'), may hold values from -0.625 to 0.625
- out_bias: bfloat16 [768], P('fsdp'), may hold values from -4 to 4
- ln2_gain: bfloat16 [768], P('fsdp'), may hold values from 0.25 to 1.75
- ln2_bias: bfloat16 [768], P('fsdp'), may hold values from -4 to 4
- w_fc1: bfloat16 [768, 3072], P('fsdp'), may hold values from -0.21875 to 0.21875
- fc1_bias: bfloat16 [3072], P('fsdp'), may hold values from -4 to 4
- w_fc2: bfloat16 [3072, 768], P('fsdp'), may hold values from -0.109375 to 0.109375
- fc2_bias: bfloat16 [768], P('fsdp'), may hold values from -4 to 4
- image_norms: bfloat16 [2, 768], P(None, 'fsdp'), may hold values from 0.25 to 1.75
- image_qkv: bfloat16 [768, 2304], P('fsdp'), may hold values from -0.21875 to 0.21875
- image_proj: bfloat16 [768, 768], P('fsdp'), may hold values from -0.625 to 0.625
- image_fc1: bfloat16 [768, 3072], P('fsdp'), may hold values from -0.21875 to 0.21875
- image_fc2: bfloat16 [3072, 768], P('fsdp'), may hold values from -0.109375 to 0.109375
Outputs:
- text_out: bfloat16 [512, 64, 768], P(('dp', 'fsdp'))
- image_out: bfloat16 [128, 50, 768], P(('dp', 'fsdp'))
- text_grad: float32 [512, 64, 768], P(('dp', 'fsdp'))
- grad_ln1_gain: float32 [768], P('fsdp')
- grad_ln1_bias: float32 [768], P('fsdp')
- grad_qkv: float32 [768, 2304], P('fsdp')
- grad_q_bias: float32 [768], P('fsdp')
- grad_v_bias: float32 [768], P('fsdp')
- grad_w_out: float32 [768, 768], P('fsdp')
- grad_out_bias: float32 [768], P('fsdp')
- grad_ln2_gain: float32 [768], P('fsdp')
- grad_ln2_bias: float32 [768], P('fsdp')
- grad_fc1: float32 [768, 3072], P('fsdp')
- grad_fc1_bias: float32 [3072], P('fsdp')
- grad_fc2: float32 [3072, 768], P('fsdp')
- grad_fc2_bias: float32 [768], P('fsdp')
Inputs may be any that keep to these rules, and one draw needn't show every extreme that they name: `text_segments`: along each row ids never fall; each id covers 1 to 32 positions and every id from 0 to 8 appears in every row.
All inputs are finite; a program needn't handle non-finite values.
Results may differ from a plain program's by a relative error of at most 0.015.
Values may be sent and summed in bfloat16 or wider, within the bound.
No kernel may reach another device: no remote copies, remote signals or barrier semaphores. Data moves between devices by JAX's collectives and lax.ppermute only.
A program may use at most 256 MiB of HBM per device.

v0:
```python
from functools import partial

import jax
import jax.numpy as jnp
from jax import lax
from jax.experimental import pallas as pl
from jax.experimental.pallas import tpu as pltpu
from jax.sharding import PartitionSpec as P

HEADS = 12
EPSILON = 1e-06
LANES = 128
TILE = 256
MIB = 1024 * 1024
F32 = jnp.float32
BF16 = jnp.bfloat16

LN1_GAIN, LN1_BIAS, Q_BIAS, V_BIAS, OUT_BIAS, LN2_GAIN, LN2_BIAS, FC2_BIAS = range(8)
IMAGE_GAIN_ONE, IMAGE_GAIN_TWO, FC1_BIAS = 8, 9, 10
VECTOR_ROWS = 16


def dot_nn(a, b):
    return lax.dot_general(a, b, (((1,), (0,)), ((), ())), preferred_element_type=F32)


def dot_nt(a, b):
    return lax.dot_general(a, b, (((1,), (1,)), ((), ())), preferred_element_type=F32)


def dot_tn(a, b):
    return lax.dot_general(a, b, (((0,), (0,)), ((), ())), preferred_element_type=F32)


def call(body, name, flops, moved, operands, after=(), num_prefetch=0, weight=1, **kwargs):
    grid_spec = kwargs.pop("grid_spec")
    first = num_prefetch + len(grid_spec["in_specs"])

    def ordered(*refs):
        return body(*refs[:first], *refs[first + len(after) :])

    grid_spec["in_specs"] = list(grid_spec["in_specs"]) + [
        pl.BlockSpec(memory_space=pltpu.HBM)
    ] * len(after)
    return pl.pallas_call(
        ordered,
        name=name,
        grid_spec=pltpu.PrefetchScalarGridSpec(num_scalar_prefetch=num_prefetch, **grid_spec),
        compiler_params=pltpu.CompilerParams(vmem_limit_bytes=63 * MIB),
        cost_estimate=pl.CostEstimate(
            flops=int(flops) * weight, bytes_accessed=int(moved), transcendentals=0
        ),
        **kwargs,
    )(*operands, *after)


class Part:
    def __init__(self, name, start, width, folds):
        self.name, self.start, self.width, self.folds = name, start, width, folds


def pack_parts(shapes):
    parts, at = {}, 0
    for name, (rows, columns), model in shapes:
        folds = rows // model
        parts[name] = Part(name, at, columns // 2, folds)
        at += folds * (columns // 2)
    return parts, at


def cut_body(plan, at, place, *refs):
    vectors, refs = (refs[0], refs[1:]) if at is not None else (None, refs)
    sources, outs = refs[: len(plan)], refs[len(plan) :]
    for source, (target, part) in zip(sources, plan):
        step = source.shape[0] // part.folds
        for fold in range(part.folds):
            left = part.start + fold * part.width
            outs[target][:, left : left + part.width] = source[fold * step : (fold + 1) * step, :]
    if vectors is None:
        return
    block = jnp.zeros((outs[0].shape[0], LANES), BF16)
    outs[0][:, at : at + LANES] = block
    outs[0][: vectors.shape[0], at : at + LANES] = vectors[...]


def cut_pieces(place, vectors, packs, after=()):
    plan, sources, shapes, specs = [], [], [], []
    for target, (parts, width, matrices) in enumerate(packs):
        for name, part in parts.items():
            plan.append((target, part))
            sources.append(matrices[name])
            rows = matrices[name].shape[0] // 2
            specs.append(pl.BlockSpec((rows, part.width), lambda i, place: (place[1], place[2])))
        width += LANES if vectors is not None else 0
        shapes.append(jax.ShapeDtypeStruct((rows // part.folds, width), BF16))
    return call(
        partial(cut_body, plan, None if vectors is None else packs[0][1]),
        "cut_pieces",
        0,
        sum(a.size for a in sources),
        (place, *([] if vectors is None else [vectors]), *sources),
        after=after,
        weight=1,
        num_prefetch=1,
        grid_spec=dict(
            grid=(1,),
            in_specs=(
                []
                if vectors is None
                else [pl.BlockSpec(vectors.shape, lambda i, place: (0, 0))]
            )
            + specs,
            out_specs=[pl.BlockSpec(a.shape, lambda i, place: (0, 0)) for a in shapes],
        ),
        out_shape=shapes,
    )


class Whole:
    def __init__(self, arrays):
        self.arrays = arrays

    def operands(self, names):
        self.asked = list(names)
        return [self.arrays[name] for name in names]

    def start(self, refs, place, names, targets, semaphores):
        for name in names:
            ref = refs[self.asked.index(name)]
            pltpu.make_async_copy(ref, targets[name], semaphores[name]).start()


def start_piece(source, parts, names, targets, semaphores, f, x, core):
    for name in names:
        part = parts[name]
        height = source.shape[0]
        first = f * (2 * part.folds * height) + x * (part.folds * height)
        for fold in range(part.folds):
            columns = part.start + fold * part.width
            pltpu.make_async_copy(
                source.at[:, pl.ds(columns, part.width)],
                targets[name].at[
                    pl.ds(pl.multiple_of(first + fold * height, 16), height),
                    pl.ds(pl.multiple_of(core * part.width, LANES), part.width),
                ],
                semaphores[name],
            ).start()


class Relative:
    def __init__(self, parts, buffers):
        self.parts, self.buffers = parts, buffers

    def operands(self, names):
        return [array for array, _ in self.buffers]

    def start(self, refs, place, names, targets, semaphores):
        f, x, core = place
        for ref, (_, (dy, dx, dc)) in zip(refs, self.buffers):
            for dz in range(ref.shape[0]):
                start_piece(
                    ref.at[dz],
                    self.parts,
                    names,
                    targets,
                    semaphores,
                    f ^ (dy + 2 * dz),
                    x ^ dx,
                    core ^ dc,
                )


class Listed:
    def __init__(self, parts, array):
        self.parts, self.array = parts, array

    def operands(self, names):
        return [self.array]

    def start(self, refs, place, names, targets, semaphores):
        (ref,) = refs

        def step(i, carry):
            start_piece(
                ref.at[i], self.parts, names, targets, semaphores, i // 4, (i // 2) % 2, i % 2
            )
            return carry

        lax.fori_loop(0, ref.shape[0], step, 0)


class Loader:
    def __init__(self, wanted, shapes):
        self.wanted, self.shapes = wanted, shapes
        self.names = [name for _, names in wanted for name in names]
        self.arrays = [a for source, names in wanted for a in source.operands(names)]
        self.specs = [pl.BlockSpec(memory_space=pltpu.HBM)] * len(self.arrays)
        self.scratch = [pltpu.VMEM(shapes[name], BF16) for name in self.names] + [
            pltpu.SemaphoreType.DMA((len(self.names),))
        ]
        self.bytes = sum(2 * shapes[name][0] * shapes[name][1] for name in self.names)

    def bind(self, refs, scratch, place_ref):
        self.refs = refs
        self.targets = dict(zip(self.names, scratch))
        self.semaphores = {name: scratch[-1].at[i] for i, name in enumerate(self.names)}
        self.place = (place_ref[0], place_ref[1], place_ref[2])
        return self

    def start(self, only=None):
        at = 0
        for source, names in self.wanted:
            count = len(source.operands(names))
            refs = self.refs[at : at + count]
            at += count
            names = [name for name in names if only is None or name in only]
            if names:
                source.start(refs, self.place, names, self.targets, self.semaphores)

    def wait(self, name):
        target = self.targets[name]
        pltpu.make_async_copy(target, target, self.semaphores[name]).wait()


def normed(values, gain, shift):
    centre = values - jnp.mean(values, axis=-1, keepdims=True)
    spread = lax.rsqrt(jnp.mean(centre * centre, axis=-1, keepdims=True) + EPSILON)
    return centre * spread * gain + shift


def norm_back(values, gain, grad):
    centre = values - jnp.mean(values, axis=-1, keepdims=True)
    spread = lax.rsqrt(jnp.mean(centre * centre, axis=-1, keepdims=True) + EPSILON)
    scaled = centre * spread
    grad_gain = jnp.sum(grad * scaled, axis=0, keepdims=True)
    grad_shift = jnp.sum(grad, axis=0, keepdims=True)
    inner = grad * gain
    inner = inner - jnp.mean(inner, axis=-1, keepdims=True) - scaled * jnp.mean(
        inner * scaled, axis=-1, keepdims=True
    )
    return inner * spread, grad_gain, grad_shift


def lane_sides(scale=1.0):
    lane = lax.broadcasted_iota(jnp.int32, (LANES, LANES), 1)
    left = jnp.where(lane < LANES // 2, scale, 0.0)
    return left.astype(BF16), (scale - left).astype(BF16)


def by_head(values, sides):
    return jnp.concatenate([values * sides[0], values * sides[1]], axis=0)


def pair_columns(width, pair):
    return [slice(third * width + pair * LANES, third * width + (pair + 1) * LANES) for third in range(3)]


def head_ones():
    row = lax.broadcasted_iota(jnp.int32, (2 * LANES, LANES), 0)
    lane = lax.broadcasted_iota(jnp.int32, (2 * LANES, LANES), 1)
    return jnp.where((row < LANES) == (lane < LANES // 2), 1.0, 0.0).astype(BF16)


def spread_ones():
    row = lax.broadcasted_iota(jnp.int32, (2 * LANES, 2 * LANES), 0)
    lane = lax.broadcasted_iota(jnp.int32, (2 * LANES, 2 * LANES), 1)
    return jnp.where((row % LANES < LANES // 2) == (lane < LANES), 1.0, 0.0).astype(BF16)


def attention(joined_ref, rows, width, allowed, store):
    sides, key_sides = lane_sides(), lane_sides((width // HEADS) ** -0.5)
    places = [pair_columns(width, pair) for pair in range(width // LANES)]
    scores = [
        dot_nt(joined_ref[rows, one], by_head(joined_ref[rows, two], key_sides))
        for one, two, _ in places
    ]
    weights = []
    for both in scores:
        parts = []
        for head in range(2):
            own = jnp.where(allowed, both[:, head * LANES : (head + 1) * LANES], -1e30)
            raised = jnp.exp(own - jnp.max(own, axis=-1, keepdims=True))
            parts.append(raised * (1.0 / jnp.sum(raised, axis=-1, keepdims=True)))
        weights.append(jnp.concatenate(parts, axis=1).astype(BF16))
    for pair, (low, (_, _, three)) in enumerate(zip(weights, places)):
        store(pair, low, by_head(joined_ref[rows, three], sides))


def gelu_both(values):
    below = 0.5 + 0.5 * lax.erf(values * 0.7071067811865476)
    bell = jnp.exp(values * values * -0.5) * 0.3989422804014327
    return values * below, below + values * bell


def text_attend_body(loader, n_sources, width, place, x_ref, ids_ref, vec_ref, *rest):
    sources, rest = rest[:n_sources], rest[n_sources:]
    pair_ref, joined_ref, weights_ref, exact_ref = rest[:4]
    load = loader.bind(sources, rest[4:], place)

    @pl.when(pl.program_id(0) == 0)
    def _():
        load.start()
        load.wait("qkv")

    w_qkv = load.targets["qkv"]
    values = x_ref[...].astype(F32)
    norm_one = normed(
        values, vec_ref[LN1_GAIN : LN1_GAIN + 1, :], vec_ref[LN1_BIAS : LN1_BIAS + 1, :]
    ).astype(BF16)
    pair_ref[:, :width] = norm_one
    for third, bias in enumerate((Q_BIAS, None, V_BIAS)):
        columns = slice(third * width, (third + 1) * width)
        product = dot_nn(norm_one, w_qkv[:, columns])
        if bias is not None:
            product = product + vec_ref[bias : bias + 1, :]
        joined_ref[:, columns] = product.astype(BF16)
    ones = head_ones()
    for part in range(x_ref.shape[0] // LANES):
        rows = slice(part * LANES, (part + 1) * LANES)
        ids = jnp.broadcast_to(ids_ref[part], (LANES, LANES))

        def store(pair, low, values):
            lanes = slice(pair * LANES, (pair + 1) * LANES)
            weights_ref[part, pair] = low
            both = dot_nn(low, jnp.concatenate([values, ones], axis=1))
            later = slice(width + pair * LANES, width + (pair + 1) * LANES)
            pair_ref[rows, later] = both[:, :LANES].astype(BF16)
            exact_ref[rows, lanes] = both[:, :LANES] / both[:, LANES:]

        attention(joined_ref, rows, width, ids == ids.T, store)


def text_forward_body(loader, n_sources, place, x_ref, mixed_ref, vec_ref, fc1_bias_ref, *rest):
    sources, rest = rest[:n_sources], rest[n_sources:]
    hidden_ref, active_ref, slope_ref = rest[:3]
    load = loader.bind(sources, rest[3:], place)
    first = pl.program_id(0) == 0

    @pl.when(first)
    def _():
        load.start(["out"])
        load.wait("out")
        load.start(["fc1"])

    hidden = (
        x_ref[...].astype(F32)
        + dot_nn(mixed_ref[...], load.targets["out"][...])
        + vec_ref[OUT_BIAS : OUT_BIAS + 1, :]
    )
    hidden_ref[...] = hidden
    norm_two = normed(
        hidden, vec_ref[LN2_GAIN : LN2_GAIN + 1, :], vec_ref[LN2_BIAS : LN2_BIAS + 1, :]
    ).astype(BF16)
    active_ref[:, slope_ref.shape[1] :] = norm_two

    @pl.when(first)
    def _():
        load.wait("fc1")

    w_fc1 = load.targets["fc1"]
    step = hidden.shape[1]
    for k in range(w_fc1.shape[1] // step):
        columns = slice(k * step, (k + 1) * step)
        pre_act = dot_nn(norm_two, w_fc1[:, columns]) + fc1_bias_ref[:, columns]
        active, slope = gelu_both(pre_act)
        active_ref[:, columns] = active.astype(BF16)
        slope_ref[:, columns] = slope.astype(BF16)


def text_back_body(loader, n_sources, place, g_ref, hidden_ref, slope_ref, vec_ref, *rest):
    sources, rest = rest[:n_sources], rest[n_sources:]
    pre_ref, share_ref, d_hidden_ref, d_mixed_ref, sums_ref, wide_ref = rest[:6]
    load = loader.bind(sources, rest[6:], place)
    first = pl.program_id(0) == 0

    @pl.when(first)
    def _():
        load.start(["fc2"])
        sums_ref[...] = jnp.zeros_like(sums_ref)
        wide_ref[...] = jnp.zeros_like(wide_ref)
        load.wait("fc2")
        load.start(["fc1", "out"])

    g = g_ref[...]
    w_fc2 = load.targets["fc2"]
    step = g.shape[1]
    for k in range(slope_ref.shape[1] // step):
        columns = slice(k * step, (k + 1) * step)
        low = (dot_nt(g, w_fc2[columns, :]) * slope_ref[:, columns].astype(F32)).astype(BF16)
        pre_ref[:, columns] = low
        half = slope_ref.shape[1] // 2

        @pl.when(place[2] != k * step // half)
        def _():
            share_ref[:, k * step % half : k * step % half + step] = low

        wide_ref[0:1, columns] += jnp.sum(low.astype(F32), axis=0, keepdims=True)

    @pl.when(first)
    def _():
        load.wait("fc1")
        load.wait("out")

    d_norm = dot_nt(pre_ref[...], load.targets["fc1"][...])
    part, gain, shift = norm_back(
        hidden_ref[...], vec_ref[LN2_GAIN : LN2_GAIN + 1, :], d_norm
    )
    d_hidden = g.astype(F32) + part
    d_hidden_ref[...] = d_hidden
    dy1 = d_hidden.astype(BF16)
    share_ref[:, slope_ref.shape[1] // 2 :] = dy1
    d_mixed_ref[...] = dot_nt(dy1, load.targets["out"][...]).astype(BF16)
    sums_ref[LN2_GAIN : LN2_GAIN + 1, :] += gain
    sums_ref[LN2_BIAS : LN2_BIAS + 1, :] += shift
    sums_ref[OUT_BIAS : OUT_BIAS + 1, :] += jnp.sum(dy1.astype(F32), axis=0, keepdims=True)
    sums_ref[FC2_BIAS : FC2_BIAS + 1, :] += jnp.sum(g.astype(F32), axis=0, keepdims=True)


def text_out_body(loader, n_sources, place, hidden_ref, active_ref, vec_ref, *rest):
    sources, rest = rest[:n_sources], rest[n_sources:]
    (out_ref,) = rest[:1]
    load = loader.bind(sources, rest[1:], place)

    @pl.when(pl.program_id(0) == 0)
    def _():
        load.start()
        load.wait("fc2")

    out_ref[...] = (
        hidden_ref[...]
        + dot_nn(active_ref[...], load.targets["fc2"][...])
        + vec_ref[FC2_BIAS : FC2_BIAS + 1, :]
    ).astype(BF16)


def text_unjoin_body(
    loader,
    n_sources,
    width,
    place,
    joined_ref,
    weights_ref,
    d_mixed_ref,
    exact_ref,
    x_ref,
    d_hidden_ref,
    vec_ref,
    begin_ref,
    *rest,
):
    sources, rest = rest[:n_sources], rest[n_sources:]
    d_joined_ref, share_ref, grad_ref, sums_ref = rest[:4]
    load = loader.bind(sources, rest[4:], place)
    start = pl.program_id(0) == 0

    @pl.when(start)
    def _():
        load.start()
        sums_ref[...] = begin_ref[...]

    scale = (width // HEADS) ** -0.5
    sides, key_sides = lane_sides(), lane_sides(scale)
    left = lax.broadcasted_iota(jnp.int32, (LANES, LANES), 1) < LANES // 2
    ones = spread_ones()
    places = [pair_columns(width, pair) for pair in range(width // LANES)]
    for part in range(joined_ref.shape[0] // LANES):
        rows = slice(part * LANES, (part + 1) * LANES)
        d_weights = [
            dot_nt(d_mixed_ref[rows, one], by_head(joined_ref[rows, three], sides))
            for one, _, three in places
        ]
        d_scores = []
        for pair, (one, _, _) in enumerate(places):
            product = d_mixed_ref[rows, one].astype(F32) * exact_ref[rows, one]
            high = product.astype(BF16)
            low = (product - high.astype(F32)).astype(BF16)
            total = dot_nn(jnp.concatenate([high, low], axis=1), ones)
            d_scores.append(
                (weights_ref[part, pair].astype(F32) * (d_weights[pair] - total)).astype(BF16)
            )
        for pair, (one, two, three) in enumerate(places):
            d_joined_ref[rows, one] = dot_nn(
                d_scores[pair], by_head(joined_ref[rows, two], key_sides)
            ).astype(BF16)
            d_keys = dot_tn(d_scores[pair], joined_ref[rows, one]) * scale
            d_joined_ref[rows, two] = jnp.where(left, d_keys[:LANES], d_keys[LANES:]).astype(BF16)
            d_values = dot_tn(weights_ref[part, pair], d_mixed_ref[rows, one])
            d_joined_ref[rows, three] = jnp.where(
                left, d_values[:LANES], d_values[LANES:]
            ).astype(BF16)
    for row, third in ((Q_BIAS, 0), (V_BIAS, 2)):
        columns = d_joined_ref[:, third * width : (third + 1) * width].astype(F32)
        sums_ref[row : row + 1, :] += jnp.sum(columns, axis=0, keepdims=True)

    @pl.when(start)
    def _():
        load.wait("qkv")

    half = share_ref.shape[1]
    theirs = pl.ds(pl.multiple_of((1 - place[2]) * half, LANES), half)
    share_ref[...] = d_joined_ref[:, theirs]
    d_norm = dot_nt(d_joined_ref[...], load.targets["qkv"][...])
    part, gain, shift = norm_back(
        x_ref[...].astype(F32), vec_ref[LN1_GAIN : LN1_GAIN + 1, :], d_norm
    )
    grad_ref[...] = d_hidden_ref[...] + part
    sums_ref[LN1_GAIN : LN1_GAIN + 1, :] += gain
    sums_ref[LN1_BIAS : LN1_BIAS + 1, :] += shift


def image_body(loader, n_sources, width, tokens, padded, place, x_ref, vec_ref, *rest):
    sources, rest = rest[:n_sources], rest[n_sources:]
    out_ref, joined_ref, mixed_ref, hidden_ref = rest[:4]
    load = loader.bind(sources, rest[4:], place)
    load.start()
    hidden_ref[...] = jnp.zeros_like(hidden_ref)
    for image in range(x_ref.shape[0]):
        hidden_ref[image * padded : image * padded + tokens, :] = x_ref[image].astype(F32)
    values = hidden_ref[...]
    norm_one = normed(values, vec_ref[IMAGE_GAIN_ONE : IMAGE_GAIN_ONE + 1, :], 0.0).astype(BF16)
    load.wait("qkv")
    w_qkv = load.targets["qkv"]
    for third in range(3):
        columns = slice(third * width, (third + 1) * width)
        joined_ref[:, columns] = dot_nn(norm_one, w_qkv[:, columns]).astype(BF16)
    row = lax.broadcasted_iota(jnp.int32, (LANES, LANES), 0)
    column = lax.broadcasted_iota(jnp.int32, (LANES, LANES), 1)
    allowed = (row // padded == column // padded) & (column % padded < tokens)
    for part in range(hidden_ref.shape[0] // LANES):
        rows = slice(part * LANES, (part + 1) * LANES)

        def store(pair, low, values):
            lanes = slice(pair * LANES, (pair + 1) * LANES)
            mixed_ref[rows, lanes] = dot_nn(low, values).astype(BF16)

        attention(joined_ref, rows, width, allowed, store)
    load.wait("out")
    hidden = values + dot_nn(mixed_ref[...], load.targets["out"][...])
    norm_two = normed(hidden, vec_ref[IMAGE_GAIN_TWO : IMAGE_GAIN_TWO + 1, :], 0.0).astype(BF16)
    hidden_ref[...] = hidden
    load.wait("fc1")
    load.wait("fc2")
    w_fc1, w_fc2 = load.targets["fc1"], load.targets["fc2"]
    for k in range(w_fc1.shape[1] // width):
        columns = slice(k * width, (k + 1) * width)
        pre_act = dot_nn(norm_two, w_fc1[:, columns])
        active = (pre_act * (0.5 + 0.5 * lax.erf(pre_act * 0.7071067811865476))).astype(BF16)
        hidden_ref[...] += dot_nn(active, w_fc2[columns, :])
    for image in range(x_ref.shape[0]):
        own = hidden_ref[image * padded : image * padded + tokens, :]
        out_ref[image] = own.astype(BF16)


SLOTS = 16
CORNERED = (0, 2, 1, 3, 4, 6, 12, 14, 9, 11, 13, 15, 5, 7, 8, 10)


class Job:
    def __init__(self, kind, lefts, rights, start, half, folds=1, wholes=(True, True)):
        self.kind, self.lefts, self.rights, self.start = kind, lefts, rights, start
        self.half, self.folds, self.wholes = half, folds, wholes
        self.width = half * folds
        self.block = half // 2 if half > 1152 else half


class Pieces:
    def __init__(self, jobs, model):
        self.jobs, self.model = jobs, model
        self.height = model // SLOTS
        self.width = sum(job.width for job in jobs)
        self.operands = []
        self.scratch = [pltpu.VMEM((SLOTS, self.height, self.width), BF16)]
        self.loads = self.flops = 0
        for job in jobs:
            self.operands += [array for array, _ in job.lefts]
            self.operands += [array for array, _ in job.rights]
            if job.kind == "sums":
                self.scratch += [
                    pltpu.VMEM((4, *job.lefts[0][0].shape), F32),
                    pltpu.VMEM((model, LANES), F32),
                ]
                self.loads += 4
                continue
            tokens = job.lefts[0][0].shape[0]
            self.scratch += [
                pltpu.VMEM((job.folds, 2 * tokens, model), BF16),
                pltpu.VMEM((2 * tokens, job.half), BF16),
                pltpu.VMEM((model, job.block), F32),
            ]
            self.loads += 2 * job.folds + 2 * job.half // job.block
            self.flops += 4 * tokens * model * job.width
        self.out_shape = [jax.ShapeDtypeStruct((4, self.height, self.width), BF16)] * 4
        self.moved = 2 * sum(a.size for a in self.operands)

    def steps(self, place, operands, outs, scratch, load, send):
        operands, scratch = list(operands), list(scratch)
        pieces = scratch.pop(0)
        steps = []
        f, x, core = place
        y, column = f % 2, f // 2
        height, model = self.height, self.model

        def put(slot, columns, value):
            pieces[CORNERED.index(slot), :, columns] = value.astype(BF16)

        def put_rows(total, columns):
            for slot in range(SLOTS):
                dy, dx, dz = slot // 8, (slot // 4) % 2, slot % 4
                first = ((f ^ (dy + 2 * dz)) * 2 + (x ^ dx)) * height
                put(slot, columns, total[pl.ds(pl.multiple_of(first, 16), height), :])
            for i, out in enumerate(outs):
                send(pieces.at[pl.ds(4 * i, 4), :, columns], out.at[:, :, columns])

        def rows_step(job, left, right, total, at):
            def compute():
                total[...] = dot_tn(left[0], right[:, at : at + job.block])
                put_rows(total, slice(job.start + at, job.start + at + job.block))

            return compute

        def folds_step(job, left, right, total, dz):
            rows = total.shape[0] // 2

            def compute():
                total[...] = dot_tn(left[dz], right[...])
                for dy in range(2):
                    for dx in range(2):
                        slot = dy * 8 + dx * 4 + dz
                        first = (y ^ dy) * rows + (x ^ dx) * (rows // 2)
                        for fold in range(job.folds):
                            lane = job.start + fold * job.half
                            top = pl.multiple_of(first + fold * height, 16)
                            put(slot, slice(lane, lane + job.half), total[pl.ds(top, height), :])
                        at = CORNERED.index(slot)
                        columns = slice(job.start, job.start + job.width)
                        send(pieces.at[at, :, columns], outs[at // 4].at[at % 4, :, columns])

            return compute

        def sums_step(job, table, total):
            def compute():
                own = jnp.where(core == 0, table[0] + table[1], table[2] + table[3])
                total[...] = jnp.concatenate([own] * (LANES // 8)).T
                put_rows(total, slice(job.start, job.start + LANES))

            return compute

        for job in self.jobs:
            left_refs = operands.pop(0), operands.pop(0)
            right_refs = operands.pop(0), operands.pop(0)
            if job.kind == "sums":
                table, total = scratch.pop(0), scratch.pop(0)
                loads = [load(ref, table.at[i]) for i, ref in enumerate(left_refs + right_refs)]
                steps.append((loads, sums_step(job, table, total)))
                continue
            left, right, total = scratch.pop(0), scratch.pop(0), scratch.pop(0)
            tokens = left.shape[1] // 2

            def load_left(fold, lane):
                return [
                    load(
                        ref.at[:, pl.ds(pl.multiple_of(first + lane, LANES), model)],
                        left.at[fold, pl.ds(i * tokens, tokens)],
                    )
                    for i, (ref, (_, first)) in enumerate(zip(left_refs, job.lefts))
                ]

            def load_right(at):
                copies = []
                for i, (ref, (_, first), both) in enumerate(
                    zip(right_refs, job.rights, job.wholes)
                ):
                    lane = first + at + (core * job.half if both else 0)
                    copies.append(
                        load(
                            ref.at[:, pl.ds(pl.multiple_of(lane, LANES), job.block)],
                            right.at[pl.ds(i * tokens, tokens), pl.ds(at, job.block)],
                        )
                    )
                return copies

            if job.kind == "folds":
                begin = load_right(0)
                for dz in range(job.folds):
                    steps.append(
                        (
                            begin + load_left(dz, (column ^ dz) * model),
                            folds_step(job, left, right, total, dz),
                        )
                    )
                    begin = []
                continue
            begin = load_left(0, 0)
            for at in range(0, job.half, job.block):
                steps.append((begin + load_right(at), rows_step(job, left, right, total, at)))
                begin = []
        return steps


class Adds:
    def __init__(self, groups):
        self.groups = groups
        self.operands, self.scratch, self.out_shape = [], [], []
        for sums in groups:
            count, height = sums[0][0][2], sums[0][0][0].shape[1]
            width = sum(pieces[0][0].shape[2] for pieces in sums)
            for pieces in sums:
                for piece in pieces:
                    self.operands.append(piece[0])
                    self.scratch.append(
                        pltpu.VMEM((count, height, pieces[0][0].shape[2]), BF16)
                    )
            self.out_shape.append(jax.ShapeDtypeStruct((count, height, width), BF16))
        self.scratch += [pltpu.VMEM(a.shape, BF16) for a in self.out_shape]
        self.loads = len(self.operands)
        self.flops = sum(a.size for a in self.out_shape)
        self.moved = 2 * sum(a.size for a in self.out_shape) * 4

    def steps(self, place, operands, outs, scratch, load, send):
        operands, scratch = list(operands), list(scratch)
        totals = scratch[len(operands) :]
        loads, work = [], []
        for sums, out, total in zip(self.groups, outs, totals):
            at = 0
            for pieces in sums:
                held = []
                for _, first, count, *lane in pieces:
                    source, target = operands.pop(0), scratch.pop(0)
                    lanes = pl.ds(lane[0] if lane else 0, target.shape[2])
                    loads.append(load(source.at[pl.ds(first, count), :, lanes], target))
                    held.append(target)
                work.append((held, total, slice(at, at + held[0].shape[2])))
                at += held[0].shape[2]

        def compute():
            for held, total, columns in work:
                value = held[0][...].astype(F32)
                for other in held[1:]:
                    value = value + other[...].astype(F32)
                total[:, :, columns] = value.astype(BF16)
            for out, total in zip(outs, totals):
                send(total, out)

        return [(loads, compute)]


def tasks_body(tasks, counts, place, *refs):
    n_in, n_out = sum(c[0] for c in counts), sum(c[1] for c in counts)
    ins, outs, held = refs[:n_in], refs[n_in : n_in + n_out], refs[n_in + n_out :]
    (in_sem, out_sem), held = held[:2], held[2:]
    where = (place[0], place[1], place[2])
    n_loads = 0

    def load(source, target):
        nonlocal n_loads
        copy = pltpu.make_async_copy(source, target, in_sem.at[n_loads])
        n_loads += 1
        return copy

    def send(source, target):
        pltpu.make_async_copy(source, target, out_sem).start()

    steps, at_in, at_out, at_held = [], 0, 0, 0
    for task, (a, b, c) in zip(tasks, counts):
        steps += task.steps(
            where,
            ins[at_in : at_in + a],
            outs[at_out : at_out + b],
            held[at_held : at_held + c],
            load,
            send,
        )
        at_in, at_out, at_held = at_in + a, at_out + b, at_held + c
    ahead = 1 if any(isinstance(task, Pieces) for task in tasks) else len(steps)
    for loads, _ in steps[:ahead]:
        for copy in loads:
            copy.start()
    for index, (loads, compute) in enumerate(steps):
        for copy in loads:
            copy.wait()
        for later, _ in steps[index + ahead : index + ahead + 1]:
            for copy in later:
                copy.start()
        compute()
    for out in outs:
        pltpu.make_async_copy(out, out, out_sem).wait()


def do_tasks(place, tasks, name, after=(), weight=1):
    counts = [(len(t.operands), len(t.out_shape), len(t.scratch)) for t in tasks]
    outs = call(
        partial(tasks_body, tasks, counts),
        name,
        sum(t.flops for t in tasks),
        sum(t.moved for t in tasks),
        (place, *[a for t in tasks for a in t.operands]),
        after=after,
        weight=weight,
        num_prefetch=1,
        grid_spec=dict(
            grid=(1,),
            in_specs=[pl.BlockSpec(memory_space=pl.ANY)] * sum(c[0] for c in counts),
            out_specs=[pl.BlockSpec(memory_space=pl.ANY)] * sum(c[1] for c in counts),
            scratch_shapes=[
                pltpu.SemaphoreType.DMA((sum(t.loads for t in tasks),)),
                pltpu.SemaphoreType.DMA,
            ]
            + [s for t in tasks for s in t.scratch],
        ),
        out_shape=[s for t in tasks for s in t.out_shape],
    )
    outs, results = list(outs), []
    for _, count, _ in counts:
        results.append(outs[:count])
        outs = outs[count:]
    return results


def swap(value, axis, bit):
    size = lax.axis_size(axis)
    return lax.ppermute(value, axis, [(i, i ^ bit) for i in range(size)])


def swap_corner(value):
    n = lax.axis_size("fsdp")
    pairs = [
        (d * n + i, (d ^ 2) * n + (i ^ 1)) for d in range(lax.axis_size("dp")) for i in range(n)
    ]
    return lax.ppermute(value, ("dp", "fsdp"), pairs)


def gate_body(count, *refs):
    pass


def gate(arrays, after):
    return call(
        partial(gate_body, len(arrays)),
        "gate",
        0,
        0,
        arrays,
        after=after,
        grid_spec=dict(
            grid=(1,),
            in_specs=[pl.BlockSpec(memory_space=pl.ANY)] * len(arrays),
            out_specs=[pl.BlockSpec(memory_space=pl.ANY)] * len(arrays),
        ),
        out_shape=[jax.ShapeDtypeStruct(a.shape, a.dtype) for a in arrays],
        input_output_aliases={i: i for i in range(len(arrays))},
    )


def gather_column(own):
    return jnp.stack([own] + [swap(own, "fsdp", bit) for bit in (2, 4, 6)])


def gather_pieces(column):
    return column, swap(column, "fsdp", 1), swap(column, "dp", 2), swap_corner(column)


def both_cores(here):
    places = ((0, 0), (1, 0), (0, 1), (1, 1))
    return [(a, at + (0,)) for a, at in zip(here, places)] + [
        (swap(a, "dp", 1), at + (1,)) for a, at in zip(here, places)
    ]


def gathered_vectors(buffers, rows, at, width, f):
    held = jnp.stack([buffers[i][0][:, :rows, at : at + width] for i in range(2)])
    held = held.reshape(2, 2, 2, rows, width)
    for axis, bit in ((0, 1), (1, 4), (2, 2)):
        held = jnp.where((f & bit) != 0, jnp.flip(held, axis), held)
    return held.transpose(3, 1, 2, 0, 4).reshape(rows, 8 * width)


class Reduction:
    def __init__(self, *sets):
        self.sets = [
            (own, swap(across, "dp", 2), swap(beside, "fsdp", 1), later)
            for own, across, beside, later in sets
        ]

    def corners(self):
        return Adds(
            [
                [[(later, 0, 2), (beside, 2, 2)] for _, _, beside, later in self.sets],
                [[(later, 2, 2), (across, 2, 2)] for _, across, _, later in self.sets],
            ]
        )

    def after_corners(self, outs):
        x_odd, y_even = outs
        self.x_odd, self.y_even = swap(x_odd, "dp", 2), swap(y_even, "fsdp", 1)

    def sides(self, straight=False):
        groups = []
        for odd in range(2):
            for at, count in ((0, 1), (1, 1)) if straight else ((0, 2),):
                sums, lane = [], 0
                for own, across, beside, _ in self.sets:
                    width = own.shape[2]
                    near, far = (beside, self.x_odd) if odd else (across, self.y_even)
                    sums.append(
                        [
                            (own, 2 * odd + at, count),
                            (near, at, count),
                            (far, at, count, lane),
                        ]
                    )
                    lane += width
                groups.append(sums)
        return Adds(groups)

    def after_sides(self, outs):
        self.low, high = outs
        self.high = swap(high, "fsdp", 2)

    def halves(self):
        return Adds([[[(self.low, i, 1), (self.high, i, 1)]] for i in range(2)])

    def after_halves(self, outs):
        own, send = outs
        self.last = [own, swap(send, "fsdp", 4)]

    def after_sides_straight(self, outs):
        own, two, one, three = outs
        self.last = [own, swap(one, "fsdp", 2), swap(two, "fsdp", 4), swap(three, "fsdp", 6)]

    def column(self):
        return [(a, 0, 1) for a in self.last]


def replicas(total):
    total = total[0]
    across = swap(total, "dp", 2)
    return total, across, swap(total, "dp", 1), swap(across, "dp", 1)


def finish_body(lots, place, *refs):
    refs, outs = refs[: 4 * len(lots)], list(refs[4 * len(lots) :])
    x_first, core_first = place[1] == 0, place[2] == 0
    for parts in lots:
        own_ref, across_ref, other_ref, diagonal_ref = refs[:4]
        refs = refs[4:]
        sides = []
        for mine, theirs in ((own_ref, across_ref), (other_ref, diagonal_ref)):
            mine, theirs = mine[...].astype(F32), theirs[...].astype(F32)
            sides.append((jnp.where(x_first, mine, theirs), jnp.where(x_first, theirs, mine)))
        at = 0
        for width, folds in parts:
            out = outs.pop(0)
            height = own_ref.shape[0]
            for dx in range(2):
                one, two = sides[0][dx], sides[1][dx]
                for fold in range(folds):
                    lanes = slice(at + fold * width, at + (fold + 1) * width)
                    rows = slice((dx * folds + fold) * height, (dx * folds + fold + 1) * height)
                    out[rows, :width] = jnp.where(core_first, one[:, lanes], two[:, lanes])
                    out[rows, width:] = jnp.where(core_first, two[:, lanes], one[:, lanes])
            at += width * folds


def finish(place, lots, parts):
    arrays = [a for lot in lots for a in lot]
    height = arrays[0].shape[0]
    shapes = [(2 * folds * height, 2 * columns) for lot in parts for columns, folds in lot]
    return call(
        partial(finish_body, parts),
        "finish",
        0,
        sum(a.size for a in arrays) * 6,
        (place, *arrays),
        num_prefetch=1,
        grid_spec=dict(
            grid=(1,),
            in_specs=[pl.BlockSpec(a.shape, lambda i, place: (0, 0)) for a in arrays],
            out_specs=[pl.BlockSpec(shape, lambda i, place: (0, 0)) for shape in shapes],
        ),
        out_shape=[jax.ShapeDtypeStruct(shape, F32) for shape in shapes],
    )


def per_device(
    text_in,
    text_segments,
    text_cotangent,
    image_in,
    ln1_gain,
    ln1_bias,
    w_qkv,
    q_bias,
    v_bias,
    w_out,
    out_bias,
    ln2_gain,
    ln2_bias,
    w_fc1,
    fc1_bias,
    w_fc2,
    fc2_bias,
    image_norms,
    image_qkv,
    image_proj,
    image_fc1,
    image_fc2,
):
    n_fsdp, n_dp = lax.axis_size("fsdp"), lax.axis_size("dp")
    batch_rows, length, model = text_in.shape
    hidden_units = w_fc1.shape[1]
    tokens = batch_rows * length
    folds = hidden_units // model
    f, replica = lax.axis_index("fsdp"), lax.axis_index("dp")
    x, core = replica // 2, replica % 2
    place = jnp.stack([f, x, core]).astype(jnp.int32)
    shard = model // n_fsdp
    by_pieces = n_fsdp == 8 and n_dp == 4 and shard % 32 == 0

    shapes = {
        "qkv": (model, 3 * model),
        "out": (model, model),
        "fc1": (model, hidden_units),
        "fc2": (hidden_units, model),
    }
    text = {"qkv": w_qkv, "out": w_out, "fc1": w_fc1, "fc2": w_fc2}
    image = {"qkv": image_qkv, "out": image_proj, "fc1": image_fc1, "fc2": image_fc2}

    def parts_of(names):
        return pack_parts([(name, shapes[name], model) for name in names])

    vectors = jnp.concatenate(
        [
            jnp.stack(
                [ln1_gain, ln1_bias, q_bias, v_bias, out_bias, ln2_gain, ln2_bias, fc2_bias]
            ),
            image_norms,
            fc1_bias.reshape(folds, shard),
        ]
    )
    vectors = jnp.pad(vectors, ((0, VECTOR_ROWS - vectors.shape[0]), (0, 0)))
    if by_pieces:
        names = ("qkv",), ("fc2",), ("out", "fc1"), ("qkv", "out", "fc1", "fc2")
        packs = [parts_of(each) + (text,) for each in names[:3]] + [parts_of(names[3]) + (image,)]
        lanes = jnp.pad(vectors, ((0, 0), (0, LANES - shard)))
        cuts = cut_pieces(place, None, packs[1:])
        cuts = cut_pieces(place, lanes, packs[:1], (cuts[0],)) + cuts
        text_qkv = Relative(packs[0][0], both_cores(gather_pieces(gather_column(cuts[0]))))
        (own,) = gate([cuts[1]], (text_qkv.buffers[0][0],))
        column_fc2 = gather_column(own)
        early = (column_fc2,)
        text_rest = Listed(packs[2][0], lax.all_gather(cuts[2], ("fsdp", "dp")))
        vectors = gathered_vectors(text_qkv.buffers, VECTOR_ROWS, packs[0][1], shard, f)
        vectors = vectors.astype(F32)
    else:
        vectors = lax.all_gather(vectors, "fsdp", axis=1, tiled=True).astype(F32)
        gathered = {n: lax.all_gather(a, "fsdp", axis=0, tiled=True) for n, a in text.items()}
        text_qkv = text_fc2 = text_rest = Whole(gathered)
        image_source = Whole(
            {n: lax.all_gather(a, "fsdp", axis=0, tiled=True) for n, a in image.items()}
        )
    fc1_vector = vectors[FC1_BIAS : FC1_BIAS + folds].reshape(folds, n_fsdp, shard)
    fc1_vector = fc1_vector.transpose(1, 0, 2).reshape(1, hidden_units)

    inflow = text_in.reshape(tokens, model)
    cotangent = text_cotangent.reshape(tokens, model)
    ids = text_segments + 16 * (lax.broadcasted_iota(jnp.int32, text_segments.shape, 0) % (LANES // length))
    ids = ids.astype(F32).reshape(tokens // LANES, 1, LANES)
    steps = tokens // TILE
    groups = TILE // LANES
    pairs = model // LANES

    def rows_of(width):
        return pl.BlockSpec((TILE, width), lambda i, place: (i, 0))

    def fixed(*shape):
        return pl.BlockSpec(shape, lambda i, place: (0,) * len(shape))

    def array(*shape, dtype=BF16):
        return jax.ShapeDtypeStruct(shape, dtype)

    weights_spec = pl.BlockSpec((groups, pairs, LANES, 2 * LANES), lambda i, place: (i, 0, 0, 0))
    vec_spec = fixed(VECTOR_ROWS, model)

    def run(body, wanted, name, flops, moved, in_specs, out_specs, out_shape, operands, grid=(steps,), extra=(), after=(), weight=1):
        loader = Loader(wanted, shapes)
        return call(
            partial(body, loader, len(loader.arrays)),
            name,
            flops,
            moved + loader.bytes,
            (place, *operands, *loader.arrays),
            after=after,
            weight=weight,
            num_prefetch=1,
            grid_spec=dict(
                grid=grid,
                in_specs=list(in_specs) + loader.specs,
                out_specs=out_specs,
                scratch_shapes=list(extra) + loader.scratch,
            ),
            out_shape=out_shape,
        )

    def bind(body, *values):
        return lambda loader, count, *refs: body(loader, count, *values, *refs)

    square = 2 * tokens * model * model
    def columns_of(width, index):
        return pl.BlockSpec((TILE, width), lambda i, place: (i, index))

    if not by_pieces:
        early = ()
    pair, joined, weights, exact = run(
        bind(text_attend_body, model),
        [(text_qkv, ["qkv"])],
        "text_attend",
        4 * square,
        tokens * model * 24,
        [rows_of(model), pl.BlockSpec((groups, 1, LANES), lambda i, place: (i, 0, 0)), vec_spec],
        [rows_of(2 * model), rows_of(3 * model), weights_spec, rows_of(model)],
        [
            array(tokens, 2 * model),
            array(tokens, 3 * model),
            array(tokens // LANES, pairs, LANES, 2 * LANES),
            array(tokens, model, dtype=F32),
        ],
        (inflow, ids, vectors),
        after=early,
    )
    done = (pair,)
    if by_pieces:
        (column_fc2,) = gate([column_fc2], done)
        pieces_fc2 = gather_pieces(column_fc2)
        their_pair, their_cotangent = swap(pair, "dp", 1), swap(cotangent, "dp", 1)
        done = (column_fc2,)
    hidden, forward, slope = run(
        text_forward_body,
        [(text_rest, ["out", "fc1"])],
        "text_forward",
        (1 + folds) * square,
        tokens * model * (10 + 4 * folds),
        [rows_of(model), columns_of(model, 1), vec_spec, fixed(1, hidden_units)],
        [rows_of(model), rows_of(hidden_units + model), rows_of(hidden_units)],
        [
            array(tokens, model, dtype=F32),
            array(tokens, hidden_units + model),
            array(tokens, hidden_units),
        ],
        (inflow, pair, vectors, fc1_vector),
        after=done,
    )
    done = (forward,)
    if by_pieces:
        *pieces_fc2, own = gate([*pieces_fc2, cuts[3]], (*done, their_pair, their_cotangent))
        image_source = Listed(packs[3][0], lax.all_gather(own, ("fsdp", "dp")))
        text_fc2 = Relative(packs[1][0], both_cores(pieces_fc2))
        (forward,) = gate([forward], [a for a, _ in text_fc2.buffers[4:]])
        done = (forward,)
        their_forward = swap(forward, "dp", 1)
    d_pre, share, d_hidden, d_mixed, sums_two, sums_wide = run(
        text_back_body,
        [(text_fc2, ["fc2"]), (text_rest, ["fc1", "out"])],
        "text_back",
        (1 + 2 * folds) * square,
        tokens * model * (16 + 4 * folds),
        [rows_of(model), rows_of(model), rows_of(hidden_units), vec_spec],
        [
            rows_of(hidden_units),
            rows_of(hidden_units // 2 + model),
            rows_of(model),
            rows_of(model),
            fixed(8, model),
            fixed(8, hidden_units),
        ],
        [
            array(tokens, hidden_units),
            array(tokens, hidden_units // 2 + model),
            array(tokens, model, dtype=F32),
            array(tokens, model),
            array(8, model, dtype=F32),
            array(8, hidden_units, dtype=F32),
        ],
        (cotangent, hidden, slope, vectors),
        after=done,
    )
    done = (d_mixed,)
    units = sums_wide[0].reshape(n_fsdp, folds, shard).transpose(1, 0, 2).reshape(folds, model)
    units = jnp.pad(units, ((0, 8 - folds), (0, 0)))
    if by_pieces:
        their_share, their_units = swap(share, "dp", 1), swap(units, "dp", 1)
        jobs = [
            Job(
                "folds",
                [(forward, 0), (their_forward, 0)],
                [(cotangent, 0), (their_cotangent, 0)],
                0,
                model // 2,
                folds,
            )
        ]
        (first,) = do_tasks(place, [Pieces(jobs, model)], "grads_one", done)
        half = hidden_units // 2
        jobs = [
            Job(
                "rows",
                [(forward, hidden_units), (their_forward, hidden_units)],
                [(d_pre, 0), (their_share, 0)],
                0,
                half,
                wholes=(True, False),
            ),
            Job(
                "rows",
                [(pair, model), (their_pair, model)],
                [(share, half), (their_share, half)],
                half,
                model // 2,
            ),
        ]
        (second,) = do_tasks(place, [Pieces(jobs, model)], "grads_two", (first[0],))
        wide = Reduction(first, second)
        done = second[0], their_units, *wide.sets[0][1:3]
    d_joined, share, text_grad, sums_one = run(
        bind(text_unjoin_body, model),
        [(text_qkv, ["qkv"])],
        "text_unjoin",
        5 * square,
        tokens * model * 32,
        [
            rows_of(3 * model),
            weights_spec,
            rows_of(model),
            rows_of(model),
            rows_of(model),
            rows_of(model),
            vec_spec,
            fixed(8, model),
        ],
        [rows_of(3 * model), rows_of(3 * model // 2), rows_of(model), fixed(8, model)],
        [
            array(tokens, 3 * model),
            array(tokens, 3 * model // 2),
            array(tokens, model, dtype=F32),
            array(8, model, dtype=F32),
        ],
        (joined, weights, d_mixed, exact, inflow, d_hidden, vectors, sums_two),
        after=done,
    )
    done = (text_grad,)
    if by_pieces:
        their_share, their_sums = swap(share, "dp", 1), swap(sums_one, "dp", 1)
    text_out = run(
        text_out_body,
        [(text_fc2, ["fc2"])],
        "text_out",
        folds * square,
        tokens * model * (6 + 2 * folds),
        [rows_of(model), rows_of(hidden_units), vec_spec],
        rows_of(model),
        array(tokens, model),
        (hidden, forward, vectors),
        after=done,
    )
    done = (text_out,)
    if by_pieces:
        (outs,) = do_tasks(place, [wide.corners()], "sums_one", done, weight=100000)
        wide.after_corners(outs)
        jobs = [
            Job(
                "rows",
                [(pair, 0), (their_pair, 0)],
                [(d_joined, 0), (their_share, 0)],
                0,
                3 * model // 2,
                wholes=(True, False),
            ),
            Job(
                "sums",
                [(sums_one, 0), (their_sums, 0)],
                [(units, 0), (their_units, 0)],
                3 * model // 2,
                LANES,
            ),
        ]
        (slots,) = do_tasks(place, [Pieces(jobs, model)], "grads_three", (outs[0],))
        narrow = Reduction(slots)
        (outs,) = do_tasks(place, [wide.sides()], "sums_two", (slots[0],))
        wide.after_sides(outs)
        done = (outs[0],)

    images, image_tokens, _ = image_in.shape
    padded = -(-image_tokens // 64) * 64
    held = images * padded
    image_out = run(
        bind(image_body, model, image_tokens, padded),
        [(image_source, ["qkv", "out", "fc1", "fc2"])],
        "image_block",
        2 * held * model * model * (4 + 2 * folds),
        4 * held * model,
        [fixed(*image_in.shape), vec_spec],
        fixed(*image_in.shape),
        array(*image_in.shape),
        (image_in, vectors),
        grid=(1,),
        extra=[
            pltpu.VMEM((held, 3 * model), BF16),
            pltpu.VMEM((held, model), BF16),
            pltpu.VMEM((held, model), F32),
        ],
        after=done,
    )
    done = (image_out,)

    if by_pieces:
        first, second = do_tasks(place, [narrow.corners(), wide.halves()], "sums_three", done)
        narrow.after_corners(first)
        wide.after_halves(second)
        (outs,) = do_tasks(place, [narrow.sides(straight=True)], "sums_four", (first[0],))
        narrow.after_sides_straight(outs)
        (((total,)),) = do_tasks(place, [Adds([[wide.column()]])], "sums_five", (outs[0],))
        early = replicas(total)
        (((total,)),) = do_tasks(place, [Adds([[narrow.column()]])], "sums_six", (total,))
        parts = ((model // 2, folds), (hidden_units // 2, 1), (model // 2, 1)), (
            (3 * model // 2, 1),
            (LANES, 1),
        )
        grad_fc2, grad_fc1, grad_out, grad_qkv, sums = finish(
            place, (early, replicas(total)), parts
        )
        sums = jnp.concatenate([sums[:, :8], sums[:, LANES : LANES + 8]], axis=1).T
    else:

        def product(left, right):
            total = lax.psum_scatter(dot_tn(left, right), "fsdp", scatter_dimension=0, tiled=True)
            return lax.psum(total, "dp")

        grad_fc2 = product(forward[:, :hidden_units], cotangent)
        grad_fc1 = product(forward[:, hidden_units:], d_pre)
        grad_out = product(pair[:, model:], d_hidden.astype(BF16))
        grad_qkv = product(pair[:, :model], d_joined)
        sums = jnp.concatenate([sums_one, units])
        sums = lax.psum_scatter(sums, "fsdp", scatter_dimension=1, tiled=True)
        sums = lax.psum(sums, "dp")

    return (
        text_out.reshape(text_in.shape),
        image_out,
        text_grad.reshape(text_in.shape),
        sums[LN1_GAIN],
        sums[LN1_BIAS],
        grad_qkv,
        sums[Q_BIAS],
        sums[V_BIAS],
        grad_out,
        sums[OUT_BIAS],
        sums[LN2_GAIN],
        sums[LN2_BIAS],
        grad_fc1,
        sums[8 : 8 + folds].reshape(-1),
        grad_fc2,
        sums[FC2_BIAS],
    )


def solution(mesh):
    rows = P(("dp", "fsdp"), None, None)
    vector, matrix = P("fsdp"), P("fsdp", None)
    in_specs = (
        rows,
        P(("dp", "fsdp"), None),
        rows,
        rows,
        vector,
        vector,
        matrix,
        vector,
        vector,
        matrix,
        vector,
        vector,
        vector,
        matrix,
        vector,
        matrix,
        vector,
        P(None, "fsdp"),
        matrix,
        matrix,
        matrix,
        matrix,
    )
    out_specs = (
        rows,
        rows,
        rows,
        vector,
        vector,
        matrix,
        vector,
        vector,
        matrix,
        vector,
        vector,
        vector,
        matrix,
        vector,
        matrix,
        vector,
    )
    return jax.shard_map(
        per_device, mesh=mesh, in_specs=in_specs, out_specs=out_specs, check_vma=False
    )
```

profile of v0, /device:TPU:11, one launch (start us, length us, event | category | flops | bytes accessed | tf_op | source)
XLA Modules:
  0.0 315.4 jit_solution(3444134681768315527)
XLA Ops:
  17.4 6.1 %collective-permute-done.2 = bf16[48,1280]{1,0:T(8,128)(2,1)S(1)} collective-permute-done((bf16[48,1280]{1,0:T(8,128)(2,1)}, bf16[48,1280]{1,0:T(8,128)(2,1)S(1)}, u32[]{:S(2)}, u32[]{:S(2)}) %collective-permute-start.2) | collective-permute-done | bytes 122912 | tf_op jit(solution)/shard_map/ppermute | solution.py:821
  23.5 3.3 %collective-permute-done.1 = bf16[48,1280]{1,0:T(8,128)(2,1)S(1)} collective-permute-done((bf16[48,1280]{1,0:T(8,128)(2,1)}, bf16[48,1280]{1,0:T(8,128)(2,1)S(1)}, u32[]{:S(2)}, u32[]{:S(2)}) %collective-permute-start.1) | collective-permute-done | bytes 122912 | tf_op jit(solution)/shard_map/ppermute | solution.py:821
  31.5 3.8 %collective-permute-start.11 = (bf16[48,1536]{1,0:T(8,128)(2,1)}, bf16[48,1536]{1,0:T(8,128)(2,1)S(1)}, u32[]{:S(2)}, u32[]{:S(2)}) collective-permute-start(bf16[48,1536]{1,0:T(8,128)(2,1)} %gate.4), channel_id=1, source_target_pairs={{0,4},{1,5},{2,6},{3,7},{4,0},{5,1},{6,2},{7,3},{8,12},{9,13},{10,... | collective-permute-start | bytes 442376 | tf_op jit(solution)/shard_map/ppermute | solution.py:821
  38.9 7.3 %collective-permute-done.11 = bf16[48,1536]{1,0:T(8,128)(2,1)S(1)} collective-permute-done((bf16[48,1536]{1,0:T(8,128)(2,1)}, bf16[48,1536]{1,0:T(8,128)(2,1)S(1)}, u32[]{:S(2)}, u32[]{:S(2)}) %collective-permute-start.11) | collective-permute-done | bytes 147488 | tf_op jit(solution)/shard_map/ppermute | solution.py:821
  55.9 3.8 %collective-permute-start.9 = (bf16[4,48,1280]{2,1,0:T(8,128)(2,1)S(1)}, bf16[4,48,1280]{2,1,0:T(8,128)(2,1)S(1)}, u32[]{:S(2)}, u32[]{:S(2)}) collective-permute-start(bf16[4,48,1280]{2,1,0:T(8,128)(2,1)S(1)} %collective-permute-done.5.refs_7_.refs_12_), channel_id=1, source_target_pairs={{0,8},{8,0},{16,24},{24,16},{1,9},{9,1},{17,25},{25,17},{2,10},{10... | collective-permute-start | bytes 1474568 | tf_op jit(solution)/shard_map/ppermute | solution.py:821
  62.6 15.8 %text_attend.1 = (bf16[1024,1536]{1,0:T(8,128)(2,1)}, bf16[1024,2304]{1,0:T(8,128)(2,1)}, bf16[8,6,128,256]{3,2,1,0:T(8,128)(2,1)}, f32[1024,768]{1,0:T(8,128)}) custom-call(s32[3]{0:T(128)} %pad_add_fusion.refs_0_, bf16[1024,768]{1,0:T(8,128)(2,1)} %bitcast.64, f32[8,1,128]{2,1,0:T(1,128)} %reshape.72.refs_2_, ...), custom_call_target="tpu_custom_call" | custom-call | flops 4831838208 | bytes 22413312 | tf_op jit(solution)/shard_map/text_attend/pallas_call | solution.py:45
  82.9 4.9 %all-gather.5.cloned.1.call-done = bf16[1536,1920]{1,0:T(8,128)(2,1)} async-done(((bf16[48,1920]{1,0:T(8,128)(2,1)}), bf16[1536,1920]{1,0:T(8,128)(2,1)}) %all-gather.5.cloned.1.call-update) | async-done | bytes 5898256 | tf_op jit(solution)/shard_map/all_gather | solution.py:1051
  87.8 19.9 %text_forward.1 = (f32[1024,768]{1,0:T(8,128)}, bf16[1024,3840]{1,0:T(8,128)(2,1)}, bf16[1024,3072]{1,0:T(8,128)(2,1)}) custom-call(s32[3]{0:T(128)} %pad_add_fusion.refs_0_, bf16[1024,768]{1,0:T(8,128)(2,1)} %bitcast.65, bf16[1024,1536]{1,0:T(8,128)(2,1)} %get-tuple-element.71.refs_1_.refs_2_.refs_5_, ...), custom_call_target="tpu_custom_call" | custom-call | flops 6039797760 | bytes 26345472 | tf_op jit(solution)/shard_map/text_forward/pallas_call | solution.py:45
  114.4 27.8 %text_back.1 = (bf16[1024,3072]{1,0:T(8,128)(2,1)}, bf16[1024,2304]{1,0:T(8,128)(2,1)}, f32[1024,768]{1,0:T(8,128)}, bf16[1024,768]{1,0:T(8,128)(2,1)}, f32[8,768]{1,0:T(8,128)}, /*index=5*/f32[8,3072]{1,0:T(8,128)}) custom-call(s32[3]{0:T(128)} %pad_add_fusion.refs_0_, bf16[1024,768]{1,0:T(8,128)(2,1)} %bitcast.62, ...), custom_call_target="tpu_custom_call" | custom-call | flops 10871635968 | bytes 35782656 | tf_op jit(solution)/shard_map/text_back/pallas_call | solution.py:45
  142.5 11.7 %grads_one.1 = (bf16[4,48,1536]{2,1,0:T(8,128)(2,1)}, bf16[4,48,1536]{2,1,0:T(8,128)(2,1)}, bf16[4,48,1536]{2,1,0:T(8,128)(2,1)}, bf16[4,48,1536]{2,1,0:T(8,128)(2,1)}) custom-call(s32[3]{0:T(128)} %pad_add_fusion.refs_0_, bf16[1024,3840]{1,0:T(8,128)(2,1)} %gate.7.refs_14_.refs_1_.refs_2_, bf16[1024,3840]{1,0:T(8,128)(2,1)} %collective-permute-done.22.refs_2_, ...), custom_call_target="tpu_custom_call" | custom-call | flops 4831838208 | bytes 18874368 | tf_op jit(solution)/shard_map/grads_one/pallas_call | solution.py:45
  158.1 16.5 %grads_two.1 = (bf16[4,48,1920]{2,1,0:T(8,128)(2,1)}, bf16[4,48,1920]{2,1,0:T(8,128)(2,1)}, bf16[4,48,1920]{2,1,0:T(8,128)(2,1)}, bf16[4,48,1920]{2,1,0:T(8,128)(2,1)}) custom-call(s32[3]{0:T(128)} %pad_add_fusion.refs_0_, bf16[1024,3840]{1,0:T(8,128)(2,1)} %gate.7.refs_14_.refs_1_.refs_2_, bf16[1024,3840]{1,0:T(8,128)(2,1)} %collective-permute-done.22.refs_2_, ...), custom_call_target="tpu_custom_call" | custom-call | flops 6039797760 | bytes 42467328 | tf_op jit(solution)/shard_map/grads_two/pallas_call | solution.py:45
  176.8 17.4 %text_unjoin.1 = (bf16[1024,2304]{1,0:T(8,128)(2,1)}, bf16[1024,1152]{1,0:T(8,128)(2,1)}, f32[1024,768]{1,0:T(8,128)}, f32[8,768]{1,0:T(8,128)}) custom-call(s32[3]{0:T(128)} %pad_add_fusion.refs_0_, bf16[1024,2304]{1,0:T(8,128)(2,1)} %get-tuple-element.80.refs_1_, bf16[8,6,128,256]{3,2,1,0:T(8,128)(2,1)} %get-tuple-element.81.refs_2_, ...), custom_call_target="tpu_custom_call" | custom-call | flops 6039797760 | bytes 28704768 | tf_op jit(solution)/shard_map/text_unjoin/pallas_call | solution.py:45
  194.7 11.6 %text_out.1.refs_9_ = bf16[1024,768]{1,0:T(8,128)(2,1)} custom-call(s32[3]{0:T(128)} %pad_add_fusion.refs_0_, f32[1024,768]{1,0:T(8,128)} %get-tuple-element.73.refs_2_.refs_1_, bf16[1024,3840]{1,0:T(8,128)(2,1)} %gate.7.refs_14_.refs_1_.refs_2_, f32[16,768]{1,0:T(8,128)} %convert_element_type.19.refs_3_.refs_4_.refs_7_.refs_2_, ...), custom_call_target="tpu_custom_call" | custom-call | flops 4831838208 | bytes 15728640 | tf_op jit(solution)/shard_map/text_out/pallas_call | solution.py:45
  209.2 3.8 %sums_one.1 = (bf16[2,48,3456]{2,1,0:T(8,128)(2,1)}, bf16[2,48,3456]{2,1,0:T(8,128)(2,1)}) custom-call(s32[3]{0:T(128)} %pad_add_fusion.refs_0_, bf16[4,48,1536]{2,1,0:T(8,128)(2,1)} %get-tuple-element.96.refs_1_.refs_5_, bf16[4,48,1536]{2,1,0:T(8,128)(2,1)} %collective-permute-done.26.refs_20_.refs_2_.refs_8_, ...), custom_call_target="tpu_custom_call" | custom-call | flops 66355200000 | bytes 5308416 | tf_op jit(solution)/shard_map/sums_one/pallas_call | solution.py:45
  218.7 10.3 %grads_three.1 = (bf16[4,48,1280]{2,1,0:T(8,128)(2,1)}, bf16[4,48,1280]{2,1,0:T(8,128)(2,1)}, bf16[4,48,1280]{2,1,0:T(8,128)(2,1)}, bf16[4,48,1280]{2,1,0:T(8,128)(2,1)}) custom-call(s32[3]{0:T(128)} %pad_add_fusion.refs_0_, bf16[1024,1536]{1,0:T(8,128)(2,1)} %get-tuple-element.71.refs_1_.refs_2_.refs_5_, ...), custom_call_target="tpu_custom_call" | custom-call | flops 3623878656 | bytes 13418496 | tf_op jit(solution)/shard_map/grads_three/pallas_call | solution.py:45
  229.9 4.2 %sums_two.1 = (bf16[2,48,3456]{2,1,0:T(8,128)(2,1)}, bf16[2,48,3456]{2,1,0:T(8,128)(2,1)}) custom-call(s32[3]{0:T(128)} %pad_add_fusion.refs_0_, bf16[4,48,1536]{2,1,0:T(8,128)(2,1)} %get-tuple-element.89.refs_9_.refs_1_.refs_7_, bf16[4,48,1536]{2,1,0:T(8,128)(2,1)} %copy-done.4, bf16[2,48,3456]{2,1,0:T(8,128)(2,1)} %copy-done.3, ...), custom_call_target="tpu_custom_call" | custom-call | flops 663552 | bytes 5308416 | tf_op jit(solution)/shard_map/sums_two/pallas_call | solution.py:45
  234.1 3.5 %collective-permute-start.35 = (bf16[2,48,3456]{2,1,0:T(8,128)(2,1)}, bf16[2,48,3456]{2,1,0:T(8,128)(2,1)}, u32[]{:S(2)}, u32[]{:S(2)}) collective-permute-start(bf16[2,48,3456]{2,1,0:T(8,128)(2,1)} %get-tuple-element.110), channel_id=1, source_target_pairs={{0,2},{1,3},{2,0},{3,1},{4,6},{5,7},{6,4},{7,5},{8,10},{9,11},{10,... | collective-permute-start | bytes 1990664 | tf_op jit(solution)/shard_map/ppermute | solution.py:821
  241.4 13.5 %image_block.1.refs_9_ = bf16[4,50,768]{2,1,0:T(8,128)(2,1)} custom-call(s32[3]{0:T(128)} %pad_add_fusion.refs_0_, bf16[4,50,768]{2,1,0:T(8,128)(2,1)} %copy.63.refs_1_, f32[16,768]{1,0:T(8,128)} %convert_element_type.19.refs_3_.refs_4_.refs_7_.refs_2_, bf16[32,48,4608]{2,1,0:T(8,128)(2,1)} %bitcast.56, ...), custom_call_target="tpu_custom_call" | custom-call | flops 3623878656 | bytes 14942208 | tf_op jit(solution)/shard_map/image_block/pallas_call | solution.py:45
  255.8 3.4 %sums_three.1 = (bf16[2,48,1280]{2,1,0:T(8,128)(2,1)}, bf16[2,48,1280]{2,1,0:T(8,128)(2,1)}, bf16[1,48,3456]{2,1,0:T(8,128)(2,1)}, bf16[1,48,3456]{2,1,0:T(8,128)(2,1)}) custom-call(s32[3]{0:T(128)} %pad_add_fusion.refs_0_, bf16[4,48,1280]{2,1,0:T(8,128)(2,1)} %get-tuple-element.107.refs_1_.refs_3_, bf16[4,48,1280]{2,1,0:T(8,128)(2,1)} %copy-done, ...), custom_call_target="tpu_custom_call" | custom-call | flops 577536 | bytes 4620288 | tf_op jit(solution)/shard_map/sums_three/pallas_call | solution.py:45
  260.2 4.3 %collective-permute-done.37.refs_3_.refs_6_ = bf16[2,48,1280]{2,1,0:T(8,128)(2,1)S(1)} collective-permute-done((bf16[2,48,1280]{2,1,0:T(8,128)(2,1)}, bf16[2,48,1280]{2,1,0:T(8,128)(2,1)S(1)}, u32[]{:S(2)}, u32[]{:S(2)}) %collective-permute-start.37) | collective-permute-done | bytes 245792 | tf_op jit(solution)/shard_map/ppermute | solution.py:821
  269.1 4.1 %collective-permute-done.36.refs_2_ = bf16[1,48,3456]{2,1,0:T(8,128)(2,1)} collective-permute-done((bf16[1,48,3456]{2,1,0:T(8,128)(2,1)}, bf16[1,48,3456]{2,1,0:T(8,128)(2,1)}, u32[]{:S(2)}, u32[]{:S(2)}) %collective-permute-start.36) | collective-permute-done | bytes 331808 | tf_op jit(solution)/shard_map/ppermute | solution.py:821
  286.2 4.0 %collective-permute-done.44.refs_4_ = bf16[1,48,1280]{2,1,0:T(8,128)(2,1)} collective-permute-done((bf16[1,48,1280]{2,1,0:T(8,128)(2,1)}, bf16[1,48,1280]{2,1,0:T(8,128)(2,1)}, u32[]{:S(2)}, u32[]{:S(2)}) %collective-permute-start.44) | collective-permute-done | bytes 122912 | tf_op jit(solution)/shard_map/ppermute | solution.py:821
  296.9 3.5 %collective-permute-start.47 = (bf16[48,1280]{1,0:T(8,128)(2,1)S(1)}, bf16[48,1280]{1,0:T(8,128)(2,1)S(1)}, u32[]{:S(2)}, u32[]{:S(2)}) collective-permute-start(bf16[48,1280]{1,0:T(8,128)(2,1)S(1)} %collective-permute-done.45.refs_6_), channel_id=1, source_target_pairs={{0,8},{8,0},{16,24},{24,16},{1,9},{9,1},{17,25},{25,17},{2,10},{10... | collective-permute-start | bytes 368648 | tf_op jit(solution)/shard_map/ppermute | solution.py:821
  302.1 4.1 %finish.1 = (f32[384,768]{1,0:T(8,128)}, f32[96,3072]{1,0:T(8,128)}, f32[96,768]{1,0:T(8,128)}, f32[96,2304]{1,0:T(8,128)}, f32[96,256]{1,0:T(8,128)}) custom-call(s32[3]{0:T(128)} %pad_add_fusion.refs_0_, bf16[48,3456]{1,0:T(8,128)(2,1)} %bitcast.60, bf16[48,3456]{1,0:T(8,128)(2,1)} %copy-done.17, bf16[48,3456]{1,0:T(8,128)(2,1)} %collective-permute-done.40.refs_3_, ...), custom_call_target="tpu_custom_call" | custom-call | bytes 5455872 | tf_op jit(solution)/shard_map/finish/pallas_call | solution.py:45
  (212 shorter events, 91.7 us)
Async XLA Ops:
  7.3 80.5 %all-gather.5.cloned.1.call-start = ((), (), s32[]{:S(2)}) async-start(), calls=%async_computation | async-start | bytes 6082560 | tf_op jit(solution)/shard_map/all_gather | solution.py:1051
  10.7 230.6 %all-gather.7.cloned.1.call-start = ((), (), s32[]{:S(2)}) async-start(), calls=%async_computation.1 | async-start | bytes 14598144 | tf_op jit(solution)/shard_map/all_gather | solution.py:1155
  28.8 22.1 %collective-permute-start.3 = (bf16[4,48,1280]{2,1,0:T(8,128)(2,1)}, bf16[4,48,1280]{2,1,0:T(8,128)(2,1)S(1)}, u32[]{:S(2)}, u32[]{:S(2)}) collective-permute-start(bf16[4,48,1280]{2,1,0:T(8,128)(2,1)} %pad_maximum_fusion.1.refs_1_.refs_4_.refs_9_), channel_id=1, source_target_pairs={{0,1},{1,0},{2,3},{3,2},{4,5},{5,4},{6,7},{7,6},{8,9},{9,8},{10,11... | collective-permute-start | bytes 1474568 | tf_op jit(solution)/shard_map/ppermute | solution.py:821
  30.1 22.7 %collective-permute-start.4 = (bf16[4,48,1280]{2,1,0:T(8,128)(2,1)}, bf16[4,48,1280]{2,1,0:T(8,128)(2,1)S(1)}, u32[]{:S(2)}, u32[]{:S(2)}) collective-permute-start(bf16[4,48,1280]{2,1,0:T(8,128)(2,1)} %pad_maximum_fusion.1.refs_1_.refs_4_.refs_9_), channel_id=1, source_target_pairs={{0,16},{8,24},{16,0},{24,8},{1,17},{9,25},{17,1},{25,9},{2,18},{10... | collective-permute-start | bytes 1474568 | tf_op jit(solution)/shard_map/ppermute | solution.py:821
  30.4 25.5 %collective-permute-start.5 = (bf16[4,48,1280]{2,1,0:T(8,128)(2,1)}, bf16[4,48,1280]{2,1,0:T(8,128)(2,1)S(1)}, u32[]{:S(2)}, u32[]{:S(2)}) collective-permute-start(bf16[4,48,1280]{2,1,0:T(8,128)(2,1)} %pad_maximum_fusion.1.refs_1_.refs_4_.refs_9_), channel_id=1, source_target_pairs={{0,17},{1,16},{2,19},{3,18},{4,21},{5,20},{6,23},{7,22},{8,25},{9,... | collective-permute-start | bytes 1474568 | tf_op jit(solution)/shard_map/ppermute | solution.py:829
  78.4 30.2 %collective-permute-start.16 = (bf16[1024,1536]{1,0:T(8,128)(2,1)}, bf16[1024,1536]{1,0:T(8,128)(2,1)}, u32[]{:S(2)}, u32[]{:S(2)}) collective-permute-start(bf16[1024,1536]{1,0:T(8,128)(2,1)} %get-tuple-element.71.refs_1_.refs_2_.refs_5_), channel_id=1, source_target_pairs={{0,8},{8,0},{16,24},{24,16},{1,9},{9,1},{17,25},{25,17},{2,10},{10... | collective-permute-start | bytes 9437192 | tf_op jit(solution)/shard_map/ppermute | solution.py:821
  78.5 29.3 %collective-permute-start.17 = (bf16[1024,768]{1,0:T(8,128)(2,1)}, bf16[1024,768]{1,0:T(8,128)(2,1)}, u32[]{:S(2)}, u32[]{:S(2)}) collective-permute-start(bf16[1024,768]{1,0:T(8,128)(2,1)} %bitcast.61), channel_id=1, source_target_pairs={{0,8},{8,0},{16,24},{24,16},{1,9},{9,1},{17,25},{25,17},{2,10},{10... | collective-permute-start | bytes 4718600 | tf_op jit(solution)/shard_map/ppermute | solution.py:821
  79.0 28.8 %collective-permute-start.13 = (bf16[4,48,1536]{2,1,0:T(8,128)(2,1)}, bf16[4,48,1536]{2,1,0:T(8,128)(2,1)S(1)}, u32[]{:S(2)}, u32[]{:S(2)}) collective-permute-start(bf16[4,48,1536]{2,1,0:T(8,128)(2,1)} %gate.5.refs_6_.refs_0_), channel_id=1, source_target_pairs={{0,1},{1,0},{2,3},{3,2},{4,5},{5,4},{6,7},{7,6},{8,9},{9,8},{10,11... | collective-permute-start | bytes 1769480 | tf_op jit(solution)/shard_map/ppermute | solution.py:821
  81.0 26.8 %collective-permute-start.14 = (bf16[4,48,1536]{2,1,0:T(8,128)(2,1)}, bf16[4,48,1536]{2,1,0:T(8,128)(2,1)}, u32[]{:S(2)}, u32[]{:S(2)}) collective-permute-start(bf16[4,48,1536]{2,1,0:T(8,128)(2,1)} %gate.5.refs_6_.refs_0_), channel_id=1, source_target_pairs={{0,16},{8,24},{16,0},{24,8},{1,17},{9,25},{17,1},{25,9},{2,18},{10... | collective-permute-start | bytes 1769480 | tf_op jit(solution)/shard_map/ppermute | solution.py:821
  81.3 27.3 %collective-permute-start.15 = (bf16[4,48,1536]{2,1,0:T(8,128)(2,1)}, bf16[4,48,1536]{2,1,0:T(8,128)(2,1)}, u32[]{:S(2)}, u32[]{:S(2)}) collective-permute-start(bf16[4,48,1536]{2,1,0:T(8,128)(2,1)} %gate.5.refs_6_.refs_0_), channel_id=1, source_target_pairs={{0,17},{1,16},{2,19},{3,18},{4,21},{5,20},{6,23},{7,22},{8,25},{9,... | collective-permute-start | bytes 1769480 | tf_op jit(solution)/shard_map/ppermute | solution.py:829
  114.0 28.4 %collective-permute-start.22 = (bf16[1024,3840]{1,0:T(8,128)(2,1)}, bf16[1024,3840]{1,0:T(8,128)(2,1)}, u32[]{:S(2)}, u32[]{:S(2)}) collective-permute-start(bf16[1024,3840]{1,0:T(8,128)(2,1)} %gate.7.refs_14_.refs_1_.refs_2_), channel_id=1, source_target_pairs={{0,8},{8,0},{16,24},{24,16},{1,9},{9,1},{17,25},{25,17},{2,10},{10... | collective-permute-start | bytes 23592968 | tf_op jit(solution)/shard_map/ppermute | solution.py:821
  142.2 15.9 %collective-permute-start.23 = (bf16[1024,2304]{1,0:T(8,128)(2,1)}, bf16[1024,2304]{1,0:T(8,128)(2,1)}, u32[]{:S(2)}, u32[]{:S(2)}) collective-permute-start(bf16[1024,2304]{1,0:T(8,128)(2,1)} %get-tuple-element.88.refs_7_), channel_id=1, source_target_pairs={{0,8},{8,0},{16,24},{24,16},{1,9},{9,1},{17,25},{25,17},{2,10},{10... | collective-permute-start | bytes 14155784 | tf_op jit(solution)/shard_map/ppermute | solution.py:821
  154.2 21.8 %collective-permute-start.25 = (bf16[4,48,1536]{2,1,0:T(8,128)(2,1)}, bf16[4,48,1536]{2,1,0:T(8,128)(2,1)S(1)}, u32[]{:S(2)}, u32[]{:S(2)}) collective-permute-start(bf16[4,48,1536]{2,1,0:T(8,128)(2,1)} %get-tuple-element.92), channel_id=1, source_target_pairs={{0,16},{8,24},{16,0},{24,8},{1,17},{9,25},{17,1},{25,9},{2,18},{10... | collective-permute-start | bytes 1769480 | tf_op jit(solution)/shard_map/ppermute | solution.py:821
  154.5 21.5 %collective-permute-start.26 = (bf16[4,48,1536]{2,1,0:T(8,128)(2,1)}, bf16[4,48,1536]{2,1,0:T(8,128)(2,1)}, u32[]{:S(2)}, u32[]{:S(2)}) collective-permute-start(bf16[4,48,1536]{2,1,0:T(8,128)(2,1)} %get-tuple-element.93), channel_id=1, source_target_pairs={{0,1},{1,0},{2,3},{3,2},{4,5},{5,4},{6,7},{7,6},{8,9},{9,8},{10,11... | collective-permute-start | bytes 1769480 | tf_op jit(solution)/shard_map/ppermute | solution.py:821
  157.2 18.8 %collective-permute-start.24 = (f32[8,768]{1,0:T(8,128)S(1)}, f32[8,768]{1,0:T(8,128)S(1)}, u32[]{:S(2)}, u32[]{:S(2)}) collective-permute-start(f32[8,768]{1,0:T(8,128)S(1)} %pad.14.refs_7_), channel_id=1, source_target_pairs={{0,8},{8,0},{16,24},{24,16},{1,9},{9,1},{17,25},{25,17},{2,10},{10... | collective-permute-start | bytes 73736 | tf_op jit(solution)/shard_map/ppermute | solution.py:821
  174.6 34.5 %collective-permute-start.27 = (bf16[4,48,1920]{2,1,0:T(8,128)(2,1)}, bf16[4,48,1920]{2,1,0:T(8,128)(2,1)}, u32[]{:S(2)}, u32[]{:S(2)}) collective-permute-start(bf16[4,48,1920]{2,1,0:T(8,128)(2,1)} %get-tuple-element.98), channel_id=1, source_target_pairs={{0,1},{1,0},{2,3},{3,2},{4,5},{5,4},{6,7},{7,6},{8,9},{9,8},{10,11... | collective-permute-start | bytes 2211848 | tf_op jit(solution)/shard_map/ppermute | solution.py:821
  174.7 34.5 %collective-permute-start.28 = (bf16[4,48,1920]{2,1,0:T(8,128)(2,1)}, bf16[4,48,1920]{2,1,0:T(8,128)(2,1)}, u32[]{:S(2)}, u32[]{:S(2)}) collective-permute-start(bf16[4,48,1920]{2,1,0:T(8,128)(2,1)} %get-tuple-element.99), channel_id=1, source_target_pairs={{0,16},{8,24},{16,0},{24,8},{1,17},{9,25},{17,1},{25,9},{2,18},{10... | collective-permute-start | bytes 2211848 | tf_op jit(solution)/shard_map/ppermute | solution.py:821
  194.3 23.8 %collective-permute-start.31 = (bf16[1024,1152]{1,0:T(8,128)(2,1)}, bf16[1024,1152]{1,0:T(8,128)(2,1)}, u32[]{:S(2)}, u32[]{:S(2)}) collective-permute-start(bf16[1024,1152]{1,0:T(8,128)(2,1)} %get-tuple-element.103), channel_id=1, source_target_pairs={{0,8},{8,0},{16,24},{24,16},{1,9},{9,1},{17,25},{25,17},{2,10},{10... | collective-permute-start | bytes 7077896 | tf_op jit(solution)/shard_map/ppermute | solution.py:821
  213.0 16.1 %collective-permute-start.29 = (bf16[2,48,3456]{2,1,0:T(8,128)(2,1)}, bf16[2,48,3456]{2,1,0:T(8,128)(2,1)S(1)}, u32[]{:S(2)}, u32[]{:S(2)}) collective-permute-start(bf16[2,48,3456]{2,1,0:T(8,128)(2,1)} %get-tuple-element.100), channel_id=1, source_target_pairs={{0,1},{1,0},{2,3},{3,2},{4,5},{5,4},{6,7},{7,6},{8,9},{9,8},{10,11... | collective-permute-start | bytes 1990664 | tf_op jit(solution)/shard_map/ppermute | solution.py:821
  234.1 20.8 %collective-permute-start.35 = (bf16[2,48,3456]{2,1,0:T(8,128)(2,1)}, bf16[2,48,3456]{2,1,0:T(8,128)(2,1)}, u32[]{:S(2)}, u32[]{:S(2)}) collective-permute-start(bf16[2,48,3456]{2,1,0:T(8,128)(2,1)} %get-tuple-element.110), channel_id=1, source_target_pairs={{0,2},{1,3},{2,0},{3,1},{4,6},{5,7},{6,4},{7,5},{8,10},{9,11},{10,... | collective-permute-start | bytes 1990664 | tf_op jit(solution)/shard_map/ppermute | solution.py:821
  237.6 17.3 %collective-permute-start.33 = (bf16[4,48,1280]{2,1,0:T(8,128)(2,1)}, bf16[4,48,1280]{2,1,0:T(8,128)(2,1)S(1)}, u32[]{:S(2)}, u32[]{:S(2)}) collective-permute-start(bf16[4,48,1280]{2,1,0:T(8,128)(2,1)} %get-tuple-element.108), channel_id=1, source_target_pairs={{0,1},{1,0},{2,3},{3,2},{4,5},{5,4},{6,7},{7,6},{8,9},{9,8},{10,11... | collective-permute-start | bytes 1474568 | tf_op jit(solution)/shard_map/ppermute | solution.py:821
  238.3 16.6 %collective-permute-start.34 = (bf16[4,48,1280]{2,1,0:T(8,128)(2,1)}, bf16[4,48,1280]{2,1,0:T(8,128)(2,1)S(1)}, u32[]{:S(2)}, u32[]{:S(2)}) collective-permute-start(bf16[4,48,1280]{2,1,0:T(8,128)(2,1)} %get-tuple-element.109), channel_id=1, source_target_pairs={{0,16},{8,24},{16,0},{24,8},{1,17},{9,25},{17,1},{25,9},{2,18},{10... | collective-permute-start | bytes 1474568 | tf_op jit(solution)/shard_map/ppermute | solution.py:821
  280.2 21.8 %collective-permute-start.40 = (bf16[48,3456]{1,0:T(8,128)(2,1)}, bf16[48,3456]{1,0:T(8,128)(2,1)}, u32[]{:S(2)}, u32[]{:S(2)}) collective-permute-start(bf16[48,3456]{1,0:T(8,128)(2,1)} %bitcast.59), channel_id=1, source_target_pairs={{0,8},{8,0},{16,24},{24,16},{1,9},{9,1},{17,25},{25,17},{2,10},{10... | collective-permute-start | bytes 995336 | tf_op jit(solution)/shard_map/ppermute | solution.py:821
  283.7 18.3 %collective-permute-start.41 = (bf16[48,3456]{1,0:T(8,128)(2,1)S(1)}, bf16[48,3456]{1,0:T(8,128)(2,1)}, u32[]{:S(2)}, u32[]{:S(2)}) collective-permute-start(bf16[48,3456]{1,0:T(8,128)(2,1)S(1)} %collective-permute-done.39.refs_2_), channel_id=1, source_target_pairs={{0,8},{8,0},{16,24},{24,16},{1,9},{9,1},{17,25},{25,17},{2,10},{10... | collective-permute-start | bytes 995336 | tf_op jit(solution)/shard_map/ppermute | solution.py:821
  (64 other events, 389.6 us)
Sparse Core Ops, SparseCore 0:
  11.6 76.1 all-gather.4
  108.7 123.6 all-gather.6
where the time goes:
time: 322 us; the launch traced here: 315 us
  Pallas kernels  173 us (54%)
  starting transfers between devices  57.1 us (18%)
  waiting for transfers between devices  48.9 us (15%)
  local copies, waits for them, and re-layouts  16 us (5%)
  between operations  14.9 us (5%)
  other arithmetic  5.23 us (2%)
    pallas_call x22, Pallas kernels, call(): pl.pallas_call(ordered, name=name, grid_spec=pltpu.PrefetchScalarGridSpec...  173 us
    ppermute x46, starting transfers between devices, swap(): return lax.ppermute(value, axis, [(i, i ^ bit) for i in range(size)])  55 us
    ppermute x46, waiting for transfers between devices, swap(): return lax.ppermute(value, axis, [(i, i ^ bit) for i in range(size)])  40.1 us
    unnamed x76, local copies, waits for them, and re-layouts  8.35 us
  transfers between devices with their start and end apart: 50, of which 23 were waited for; matrix products, arithmetic and copies ran while one was open for 4% of the time, Pallas kernels for 51%

commit v1 on v0

--- a/solution.py
+++ b/solution.py
@@ -369,8 +369,8 @@
 
 def text_back_body(loader, n_sources, place, g_ref, hidden_ref, slope_ref, vec_ref, *rest):
     sources, rest = rest[:n_sources], rest[n_sources:]
-    pre_ref, share_ref, d_hidden_ref, d_mixed_ref, sums_ref, wide_ref = rest[:6]
-    load = loader.bind(sources, rest[6:], place)
+    mine_ref, share_ref, d_mixed_ref, sums_ref, wide_ref = rest[:5]
+    load = loader.bind(sources, rest[5:], place)
     first = pl.program_id(0) == 0
 
     @pl.when(first)
@@ -383,31 +383,28 @@
 
     g = g_ref[...]
     w_fc2 = load.targets["fc2"]
-    step = g.shape[1]
-    for k in range(slope_ref.shape[1] // step):
-        columns = slice(k * step, (k + 1) * step)
-        low = (dot_nt(g, w_fc2[columns, :]) * slope_ref[:, columns].astype(F32)).astype(BF16)
-        pre_ref[:, columns] = low
-        half = slope_ref.shape[1] // 2
-
-        @pl.when(place[2] != k * step // half)
-        def _():
-            share_ref[:, k * step % half : k * step % half + step] = low
-
-        wide_ref[0:1, columns] += jnp.sum(low.astype(F32), axis=0, keepdims=True)
+    step, half = g.shape[1], mine_ref.shape[1]
+    starts = [pl.multiple_of(side * half, LANES) for side in (place[2], 1 - place[2])]
+    for start, out in zip(starts, (mine_ref, share_ref)):
+        for at in range(0, half, step):
+            columns = pl.ds(pl.multiple_of(start + at, LANES), step)
+            grad = dot_nt(g, w_fc2[columns, :])
+            low = (grad * slope_ref[:, columns].astype(F32)).astype(BF16)
+            out[:, at : at + step] = low
+            wide_ref[0:1, columns] += jnp.sum(low.astype(F32), axis=0, keepdims=True)
 
     @pl.when(first)
     def _():
         load.wait("fc1")
         load.wait("out")
 
-    d_norm = dot_nt(pre_ref[...], load.targets["fc1"][...])
+    w_fc1 = load.targets["fc1"]
+    d_norm = dot_nt(mine_ref[...], w_fc1[:, pl.ds(starts[0], half)])
+    d_norm = d_norm + dot_nt(share_ref[:, :half], w_fc1[:, pl.ds(starts[1], half)])
     part, gain, shift = norm_back(
         hidden_ref[...], vec_ref[LN2_GAIN : LN2_GAIN + 1, :], d_norm
     )
-    d_hidden = g.astype(F32) + part
-    d_hidden_ref[...] = d_hidden
-    dy1 = d_hidden.astype(BF16)
+    dy1 = (g.astype(F32) + part).astype(BF16)
     share_ref[:, slope_ref.shape[1] // 2 :] = dy1
     d_mixed_ref[...] = dot_nt(dy1, load.targets["out"][...]).astype(BF16)
     sums_ref[LN2_GAIN : LN2_GAIN + 1, :] += gain
@@ -443,7 +440,7 @@
     d_mixed_ref,
     exact_ref,
     x_ref,
-    d_hidden_ref,
+    dy1_ref,
     vec_ref,
     begin_ref,
     *rest,
@@ -503,7 +500,7 @@
     part, gain, shift = norm_back(
         x_ref[...].astype(F32), vec_ref[LN1_GAIN : LN1_GAIN + 1, :], d_norm
     )
-    grad_ref[...] = d_hidden_ref[...] + part
+    grad_ref[...] = dy1_ref[...].astype(F32) + part
     sums_ref[LN1_GAIN : LN1_GAIN + 1, :] += gain
     sums_ref[LN1_BIAS : LN1_BIAS + 1, :] += shift
 
@@ -1047,7 +1044,8 @@
         text_qkv = Relative(packs[0][0], both_cores(gather_pieces(gather_column(cuts[0]))))
         (own,) = gate([cuts[1]], (text_qkv.buffers[0][0],))
         column_fc2 = gather_column(own)
-        early = (column_fc2,)
+        (image_in,) = gate([image_in], (own,))
+        early = column_fc2, image_in
         text_rest = Listed(packs[2][0], lax.all_gather(cuts[2], ("fsdp", "dp")))
         vectors = gathered_vectors(text_qkv.buffers, VECTOR_ROWS, packs[0][1], shard, f)
         vectors = vectors.astype(F32)
@@ -1157,7 +1155,7 @@
         (forward,) = gate([forward], [a for a, _ in text_fc2.buffers[4:]])
         done = (forward,)
         their_forward = swap(forward, "dp", 1)
-    d_pre, share, d_hidden, d_mixed, sums_two, sums_wide = run(
+    d_pre, share, d_mixed, sums_two, sums_wide = run(
         text_back_body,
         [(text_fc2, ["fc2"]), (text_rest, ["fc1", "out"])],
         "text_back",
@@ -1165,17 +1163,15 @@
         tokens * model * (16 + 4 * folds),
         [rows_of(model), rows_of(model), rows_of(hidden_units), vec_spec],
         [
-            rows_of(hidden_units),
+            rows_of(hidden_units // 2),
             rows_of(hidden_units // 2 + model),
-            rows_of(model),
             rows_of(model),
             fixed(8, model),
             fixed(8, hidden_units),
         ],
         [
-            array(tokens, hidden_units),
+            array(tokens, hidden_units // 2),
             array(tokens, hidden_units // 2 + model),
-            array(tokens, model, dtype=F32),
             array(tokens, model),
             array(8, model, dtype=F32),
             array(8, hidden_units, dtype=F32),
@@ -1184,6 +1180,7 @@
         after=done,
     )
     done = (d_mixed,)
+    early_share = share
     units = sums_wide[0].reshape(n_fsdp, folds, shard).transpose(1, 0, 2).reshape(folds, model)
     units = jnp.pad(units, ((0, 8 - folds), (0, 0)))
     if by_pieces:
@@ -1207,19 +1204,19 @@
                 [(d_pre, 0), (their_share, 0)],
                 0,
                 half,
-                wholes=(True, False),
-            ),
-            Job(
-                "rows",
-                [(pair, model), (their_pair, model)],
-                [(share, half), (their_share, half)],
-                half,
-                model // 2,
+                wholes=(False, False),
             ),
         ]
         (second,) = do_tasks(place, [Pieces(jobs, model)], "grads_two", (first[0],))
         wide = Reduction(first, second)
         done = second[0], their_units, *wide.sets[0][1:3]
+        out_job = Job(
+            "rows",
+            [(pair, model), (their_pair, model)],
+            [(share, half), (their_share, half)],
+            0,
+            model // 2,
+        )
     d_joined, share, text_grad, sums_one = run(
         bind(text_unjoin_body, model),
         [(text_qkv, ["qkv"])],
@@ -1232,7 +1229,7 @@
             rows_of(model),
             rows_of(model),
             rows_of(model),
-            rows_of(model),
+            columns_of(model, hidden_units // 2 // model),
             vec_spec,
             fixed(8, model),
         ],
@@ -1243,7 +1240,7 @@
             array(tokens, model, dtype=F32),
             array(8, model, dtype=F32),
         ],
-        (joined, weights, d_mixed, exact, inflow, d_hidden, vectors, sums_two),
+        (joined, weights, d_mixed, exact, inflow, share, vectors, sums_two),
         after=done,
     )
     done = (text_grad,)
@@ -1266,11 +1263,12 @@
         (outs,) = do_tasks(place, [wide.corners()], "sums_one", done, weight=100000)
         wide.after_corners(outs)
         jobs = [
+            out_job,
             Job(
                 "rows",
                 [(pair, 0), (their_pair, 0)],
                 [(d_joined, 0), (their_share, 0)],
-                0,
+                model // 2,
                 3 * model // 2,
                 wholes=(True, False),
             ),
@@ -1278,7 +1276,7 @@
                 "sums",
                 [(sums_one, 0), (their_sums, 0)],
                 [(units, 0), (their_units, 0)],
-                3 * model // 2,
+                2 * model,
                 LANES,
             ),
         ]
@@ -1317,15 +1315,18 @@
         wide.after_halves(second)
         (outs,) = do_tasks(place, [narrow.sides(straight=True)], "sums_four", (first[0],))
         narrow.after_sides_straight(outs)
-        (((total,)),) = do_tasks(place, [Adds([[wide.column()]])], "sums_five", (outs[0],))
-        early = replicas(total)
-        (((total,)),) = do_tasks(place, [Adds([[narrow.column()]])], "sums_six", (total,))
-        parts = ((model // 2, folds), (hidden_units // 2, 1), (model // 2, 1)), (
+        (((total,)),) = do_tasks(
+            place, [Adds([[wide.column(), narrow.column()]])], "sums_five", (outs[0],)
+        )
+        parts = (
+            (model // 2, folds),
+            (hidden_units // 2, 1),
+            (model // 2, 1),
             (3 * model // 2, 1),
             (LANES, 1),
         )
         grad_fc2, grad_fc1, grad_out, grad_qkv, sums = finish(
-            place, (early, replicas(total)), parts
+            place, (replicas(total),), (parts,)
         )
         sums = jnp.concatenate([sums[:, :8], sums[:, LANES : LANES + 8]], axis=1).T
     else:
@@ -1335,8 +1336,13 @@
             return lax.psum(total, "dp")
 
         grad_fc2 = product(forward[:, :hidden_units], cotangent)
+        first = replica % 2 == 0
+        mine, theirs = d_pre, early_share[:, : hidden_units // 2]
+        d_pre = jnp.concatenate(
+            [jnp.where(first, mine, theirs), jnp.where(first, theirs, mine)], axis=1
+        )
         grad_fc1 = product(forward[:, hidden_units:], d_pre)
-        grad_out = product(pair[:, model:], d_hidden.astype(BF16))
+        grad_out = product(pair[:, model:], early_share[:, hidden_units // 2 :])
         grad_qkv = product(pair[:, :model], d_joined)
         sums = jnp.concatenate([sums_one, units])
         sums = lax.psum_scatter(sums, "fsdp", scatter_dimension=1, tiled=True)

time: 322 us -> 316 us (0.981)
  starting transfers between devices: 57.1 us -> 47.8 us
  waiting for transfers between devices: 48.9 us -> 57.3 us
  Pallas kernels: 173 us -> 166 us
    ppermute x46 -> x43, starting transfers between devices: 55 us -> 45.4 us  [swap(): return lax.ppermute(value, axis, [(i, i ^ bit) for i in range(size)])]
    ppermute x46 -> x43, waiting for transfers between devices: 40.1 us -> 48.8 us  [swap(): return lax.ppermute(value, axis, [(i, i ^ bit) for i in range(size)])]
    pallas_call x22, Pallas kernels: 173 us -> 166 us  [call(): pl.pallas_call(ordered, name=name, grid_spec=pltpu.PrefetchScalarGridSpec...]
    unnamed x76 -> x66, local copies, waits for them, and re-layouts: 8.35 us -> 9.69 us
  transfers between devices with their start and end apart: 50 -> 47, of which waited for: 23 -> 20; matrix products, arithmetic and copies ran while one was open for 4% -> 5% of each run, Pallas kernels for 51% -> 49%
where the time goes in v1:
time: 316 us; the launch traced here: 311 us
  Pallas kernels  166 us (53%)
  waiting for transfers between devices  57.3 us (18%)
  starting transfers between devices  47.8 us (15%)
  local copies, waits for them, and re-layouts  17.4 us (6%)
  between operations  14.9 us (5%)
  other arithmetic  6.98 us (2%)
    pallas_call x22, Pallas kernels, call(): pl.pallas_call(ordered, name=name, grid_spec=pltpu.PrefetchScalarGridSpec...  166 us
    ppermute x43, waiting for transfers between devices, swap(): return lax.ppermute(value, axis, [(i, i ^ bit) for i in range(size)])  48.8 us
    ppermute x43, starting transfers between devices, swap(): return lax.ppermute(value, axis, [(i, i ^ bit) for i in range(size)])  45.4 us
    unnamed x66, local copies, waits for them, and re-layouts  9.69 us
  transfers between devices with their start and end apart: 47, of which 20 were waited for; matrix products, arithmetic and copies ran while one was open for 5% of the time, Pallas kernels for 49%

profile of v1, /device:TPU:11, one launch (start us, length us, event | category | flops | bytes accessed | tf_op | source)
XLA Modules:
  0.0 310.7 jit_solution(2075531739949634451)
XLA Ops:
  17.4 6.1 %collective-permute-done.2 = bf16[48,1280]{1,0:T(8,128)(2,1)S(1)} collective-permute-done((bf16[48,1280]{1,0:T(8,128)(2,1)}, bf16[48,1280]{1,0:T(8,128)(2,1)S(1)}, u32[]{:S(2)}, u32[]{:S(2)}) %collective-permute-start.2) | collective-permute-done | bytes 122912 | tf_op jit(solution)/shard_map/ppermute | solution.py:818
  23.5 3.2 %collective-permute-done.1 = bf16[48,1280]{1,0:T(8,128)(2,1)S(1)} collective-permute-done((bf16[48,1280]{1,0:T(8,128)(2,1)}, bf16[48,1280]{1,0:T(8,128)(2,1)S(1)}, u32[]{:S(2)}, u32[]{:S(2)}) %collective-permute-start.1) | collective-permute-done | bytes 122912 | tf_op jit(solution)/shard_map/ppermute | solution.py:818
  31.6 3.8 %collective-permute-start.11 = (bf16[48,1536]{1,0:T(8,128)(2,1)}, bf16[48,1536]{1,0:T(8,128)(2,1)}, u32[]{:S(2)}, u32[]{:S(2)}) collective-permute-start(bf16[48,1536]{1,0:T(8,128)(2,1)} %gate.5.refs_1_), channel_id=1, source_target_pairs={{0,4},{1,5},{2,6},{3,7},{4,0},{5,1},{6,2},{7,3},{8,12},{9,13},{10,... | collective-permute-start | bytes 442376 | tf_op jit(solution)/shard_map/ppermute | solution.py:818
  41.4 5.1 %collective-permute-done.11 = bf16[48,1536]{1,0:T(8,128)(2,1)} collective-permute-done((bf16[48,1536]{1,0:T(8,128)(2,1)}, bf16[48,1536]{1,0:T(8,128)(2,1)}, u32[]{:S(2)}, u32[]{:S(2)}) %collective-permute-start.11) | collective-permute-done | bytes 147488 | tf_op jit(solution)/shard_map/ppermute | solution.py:818
  56.1 3.8 %collective-permute-start.9 = (bf16[4,48,1280]{2,1,0:T(8,128)(2,1)}, bf16[4,48,1280]{2,1,0:T(8,128)(2,1)S(1)}, u32[]{:S(2)}, u32[]{:S(2)}) collective-permute-start(bf16[4,48,1280]{2,1,0:T(8,128)(2,1)} %collective-permute-done.5.refs_7_.refs_12_), channel_id=1, source_target_pairs={{0,8},{8,0},{16,24},{24,16},{1,9},{9,1},{17,25},{25,17},{2,10},{10... | collective-permute-start | bytes 1474568 | tf_op jit(solution)/shard_map/ppermute | solution.py:818
  64.0 15.7 %text_attend.1 = (bf16[1024,1536]{1,0:T(8,128)(2,1)}, bf16[1024,2304]{1,0:T(8,128)(2,1)}, bf16[8,6,128,256]{3,2,1,0:T(8,128)(2,1)}, f32[1024,768]{1,0:T(8,128)}) custom-call(s32[3]{0:T(128)} %pad_add_fusion.refs_0_, bf16[1024,768]{1,0:T(8,128)(2,1)} %bitcast.65, f32[8,1,128]{2,1,0:T(1,128)} %reshape.72.refs_2_, ...), custom_call_target="tpu_custom_call" | custom-call | flops 4831838208 | bytes 22413312 | tf_op jit(solution)/shard_map/text_attend/pallas_call | solution.py:45
  83.6 5.5 %all-gather.5.cloned.1.call-done = bf16[1536,1920]{1,0:T(8,128)(2,1)} async-done(((bf16[48,1920]{1,0:T(8,128)(2,1)}), bf16[1536,1920]{1,0:T(8,128)(2,1)}) %all-gather.5.cloned.1.call-update) | async-done | bytes 5898256 | tf_op jit(solution)/shard_map/all_gather | solution.py:1049
  89.1 19.9 %text_forward.1 = (f32[1024,768]{1,0:T(8,128)}, bf16[1024,3840]{1,0:T(8,128)(2,1)}, bf16[1024,3072]{1,0:T(8,128)(2,1)}) custom-call(s32[3]{0:T(128)} %pad_add_fusion.refs_0_, bf16[1024,768]{1,0:T(8,128)(2,1)} %bitcast.66, bf16[1024,1536]{1,0:T(8,128)(2,1)} %get-tuple-element.70.refs_1_.refs_2_.refs_5_, ...), custom_call_target="tpu_custom_call" | custom-call | flops 6039797760 | bytes 26345472 | tf_op jit(solution)/shard_map/text_forward/pallas_call | solution.py:45
  115.1 24.7 %text_back.1 = (bf16[1024,1536]{1,0:T(8,128)(2,1)}, bf16[1024,2304]{1,0:T(8,128)(2,1)}, bf16[1024,768]{1,0:T(8,128)(2,1)}, f32[8,768]{1,0:T(8,128)}, f32[8,3072]{1,0:T(8,128)}) custom-call(s32[3]{0:T(128)} %pad_add_fusion.refs_0_, bf16[1024,768]{1,0:T(8,128)(2,1)} %bitcast.62, f32[1024,768]{1,0:T(8,128)} %get-tuple-element.72.refs_2_.refs_1_, ...), custom_call_target="tpu_custom_call" | custom-call | flops 10871635968 | bytes 35782656 | tf_op jit(solution)/shard_map/text_back/pallas_call | solution.py:45
  140.1 12.0 %grads_one.1 = (bf16[4,48,1536]{2,1,0:T(8,128)(2,1)}, bf16[4,48,1536]{2,1,0:T(8,128)(2,1)}, bf16[4,48,1536]{2,1,0:T(8,128)(2,1)}, bf16[4,48,1536]{2,1,0:T(8,128)(2,1)}) custom-call(s32[3]{0:T(128)} %pad_add_fusion.refs_0_, bf16[1024,3840]{1,0:T(8,128)(2,1)} %gate.9.refs_14_.refs_1_.refs_2_, bf16[1024,3840]{1,0:T(8,128)(2,1)} %collective-permute-done.22.refs_2_, ...), custom_call_target="tpu_custom_call" | custom-call | flops 4831838208 | bytes 18874368 | tf_op jit(solution)/shard_map/grads_one/pallas_call | solution.py:45
  155.7 11.8 %grads_two.1 = (bf16[4,48,1536]{2,1,0:T(8,128)(2,1)}, bf16[4,48,1536]{2,1,0:T(8,128)(2,1)}, bf16[4,48,1536]{2,1,0:T(8,128)(2,1)}, bf16[4,48,1536]{2,1,0:T(8,128)(2,1)}) custom-call(s32[3]{0:T(128)} %pad_add_fusion.refs_0_, bf16[1024,3840]{1,0:T(8,128)(2,1)} %gate.9.refs_14_.refs_1_.refs_2_, bf16[1024,3840]{1,0:T(8,128)(2,1)} %collective-permute-done.22.refs_2_, ...), custom_call_target="tpu_custom_call" | custom-call | flops 4831838208 | bytes 23592960 | tf_op jit(solution)/shard_map/grads_two/pallas_call | solution.py:45
  169.9 17.3 %text_unjoin.1 = (bf16[1024,2304]{1,0:T(8,128)(2,1)}, bf16[1024,1152]{1,0:T(8,128)(2,1)}, f32[1024,768]{1,0:T(8,128)}, f32[8,768]{1,0:T(8,128)}) custom-call(s32[3]{0:T(128)} %pad_add_fusion.refs_0_, bf16[1024,2304]{1,0:T(8,128)(2,1)} %get-tuple-element.79.refs_1_, bf16[8,6,128,256]{3,2,1,0:T(8,128)(2,1)} %get-tuple-element.80.refs_2_, ...), custom_call_target="tpu_custom_call" | custom-call | flops 6039797760 | bytes 28704768 | tf_op jit(solution)/shard_map/text_unjoin/pallas_call | solution.py:45
  187.8 11.6 %text_out.1.refs_9_ = bf16[1024,768]{1,0:T(8,128)(2,1)} custom-call(s32[3]{0:T(128)} %pad_add_fusion.refs_0_, f32[1024,768]{1,0:T(8,128)} %get-tuple-element.72.refs_2_.refs_1_, bf16[1024,3840]{1,0:T(8,128)(2,1)} %gate.9.refs_14_.refs_1_.refs_2_, f32[16,768]{1,0:T(8,128)} %convert_element_type.19.refs_3_.refs_4_.refs_7_.refs_2_, ...), custom_call_target="tpu_custom_call" | custom-call | flops 4831838208 | bytes 15728640 | tf_op jit(solution)/shard_map/text_out/pallas_call | solution.py:45
  199.4 3.7 %sums_one.1 = (bf16[2,48,3072]{2,1,0:T(8,128)(2,1)}, bf16[2,48,3072]{2,1,0:T(8,128)(2,1)}) custom-call(s32[3]{0:T(128)} %pad_add_fusion.refs_0_, bf16[4,48,1536]{2,1,0:T(8,128)(2,1)} %get-tuple-element.94.refs_1_.refs_5_, bf16[4,48,1536]{2,1,0:T(8,128)(2,1)} %collective-permute-done.26.refs_20_.refs_2_.refs_8_, ...), custom_call_target="tpu_custom_call" | custom-call | flops 58982400000 | bytes 4718592 | tf_op jit(solution)/shard_map/sums_one/pallas_call | solution.py:45
  206.7 13.7 %grads_three.1 = (bf16[4,48,1664]{2,1,0:T(8,128)(2,1)}, bf16[4,48,1664]{2,1,0:T(8,128)(2,1)}, bf16[4,48,1664]{2,1,0:T(8,128)(2,1)}, bf16[4,48,1664]{2,1,0:T(8,128)(2,1)}) custom-call(s32[3]{0:T(128)} %pad_add_fusion.refs_0_, bf16[1024,1536]{1,0:T(8,128)(2,1)} %get-tuple-element.70.refs_1_.refs_2_.refs_5_, ...), custom_call_target="tpu_custom_call" | custom-call | flops 4831838208 | bytes 29147136 | tf_op jit(solution)/shard_map/grads_three/pallas_call | solution.py:45
  221.4 4.0 %sums_two.1 = (bf16[2,48,3072]{2,1,0:T(8,128)(2,1)}, bf16[2,48,3072]{2,1,0:T(8,128)(2,1)}) custom-call(s32[3]{0:T(128)} %pad_add_fusion.refs_0_, bf16[4,48,1536]{2,1,0:T(8,128)(2,1)} %get-tuple-element.87.refs_5_.refs_1_.refs_7_, bf16[4,48,1536]{2,1,0:T(8,128)(2,1)} %copy-done.4, bf16[2,48,3072]{2,1,0:T(8,128)(2,1)} %collective-permute-done.29.refs_3_.refs_6_, ...), custom_call_target="tpu_custom_call" | custom-call | flops 589824 | bytes 4718592 | tf_op jit(solution)/shard_map/sums_two/pallas_call | solution.py:45
  225.4 4.6 %collective-permute-start.35 = (bf16[2,48,3072]{2,1,0:T(8,128)(2,1)}, bf16[2,48,3072]{2,1,0:T(8,128)(2,1)}, u32[]{:S(2)}, u32[]{:S(2)}) collective-permute-start(bf16[2,48,3072]{2,1,0:T(8,128)(2,1)} %get-tuple-element.108), channel_id=1, source_target_pairs={{0,2},{1,3},{2,0},{3,1},{4,6},{5,7},{6,4},{7,5},{8,10},{9,11},{10,... | collective-permute-start | bytes 1769480 | tf_op jit(solution)/shard_map/ppermute | solution.py:818
  230.5 13.5 %image_block.1.refs_9_ = bf16[4,50,768]{2,1,0:T(8,128)(2,1)} custom-call(s32[3]{0:T(128)} %pad_add_fusion.refs_0_, bf16[4,50,768]{2,1,0:T(8,128)(2,1)} %gate.6.refs_13_.refs_1_, f32[16,768]{1,0:T(8,128)} %convert_element_type.19.refs_3_.refs_4_.refs_7_.refs_2_, bf16[32,48,4608]{2,1,0:T(8,128)(2,1)} %bitcast.55, ...), custom_call_target="tpu_custom_call" | custom-call | flops 3623878656 | bytes 14942208 | tf_op jit(solution)/shard_map/image_block/pallas_call | solution.py:45
  251.4 5.5 %collective-permute-done.37.refs_3_.refs_6_ = bf16[2,48,1664]{2,1,0:T(8,128)(2,1)S(1)} collective-permute-done((bf16[2,48,1664]{2,1,0:T(8,128)(2,1)}, bf16[2,48,1664]{2,1,0:T(8,128)(2,1)S(1)}, u32[]{:S(2)}, u32[]{:S(2)}) %collective-permute-start.37) | collective-permute-done | bytes 319520 | tf_op jit(solution)/shard_map/ppermute | solution.py:818
  258.3 3.3 %sums_four.1 = (bf16[1,48,1664]{2,1,0:T(8,128)(2,1)}, bf16[1,48,1664]{2,1,0:T(8,128)(2,1)}, bf16[1,48,1664]{2,1,0:T(8,128)(2,1)}, bf16[1,48,1664]{2,1,0:T(8,128)(2,1)}) custom-call(s32[3]{0:T(128)} %pad_add_fusion.refs_0_, bf16[4,48,1664]{2,1,0:T(8,128)(2,1)} %get-tuple-element.103.refs_13_.refs_1_.refs_4_.refs_7_.refs_10_, ...), custom_call_target="tpu_custom_call" | custom-call | flops 319488 | bytes 2555904 | tf_op jit(solution)/shard_map/sums_four/pallas_call | solution.py:45
  264.7 7.3 %collective-permute-done.39.refs_4_ = bf16[1,48,1664]{2,1,0:T(8,128)(2,1)S(1)} collective-permute-done((bf16[1,48,1664]{2,1,0:T(8,128)(2,1)}, bf16[1,48,1664]{2,1,0:T(8,128)(2,1)S(1)}, u32[]{:S(2)}, u32[]{:S(2)}) %collective-permute-start.39) | collective-permute-done | bytes 159776 | tf_op jit(solution)/shard_map/ppermute | solution.py:818
  275.0 4.1 %collective-permute-done.41.refs_6_ = bf16[1,48,1664]{2,1,0:T(8,128)(2,1)S(1)} collective-permute-done((bf16[1,48,1664]{2,1,0:T(8,128)(2,1)}, bf16[1,48,1664]{2,1,0:T(8,128)(2,1)S(1)}, u32[]{:S(2)}, u32[]{:S(2)}) %collective-permute-start.41) | collective-permute-done | bytes 159776 | tf_op jit(solution)/shard_map/ppermute | solution.py:818
  285.1 7.9 %collective-permute-done.42.refs_2_ = bf16[48,4736]{1,0:T(8,128)(2,1)S(1)} collective-permute-done((bf16[48,4736]{1,0:T(8,128)(2,1)}, bf16[48,4736]{1,0:T(8,128)(2,1)S(1)}, u32[]{:S(2)}, u32[]{:S(2)}) %collective-permute-start.42) | collective-permute-done | bytes 454688 | tf_op jit(solution)/shard_map/ppermute | solution.py:818
  297.3 4.1 %finish.1 = (f32[384,768]{1,0:T(8,128)}, f32[96,3072]{1,0:T(8,128)}, f32[96,768]{1,0:T(8,128)}, f32[96,2304]{1,0:T(8,128)}, f32[96,256]{1,0:T(8,128)}) custom-call(s32[3]{0:T(128)} %pad_add_fusion.refs_0_, bf16[48,4736]{1,0:T(8,128)(2,1)} %bitcast.60, bf16[48,4736]{1,0:T(8,128)(2,1)} %copy-done.13, bf16[48,4736]{1,0:T(8,128)(2,1)} %collective-permute-done.43.refs_3_, ...), custom_call_target="tpu_custom_call" | custom-call | bytes 5455872 | tf_op jit(solution)/shard_map/finish/pallas_call | solution.py:45
  (196 shorter events, 83.8 us)
Async XLA Ops:
  7.3 81.8 %all-gather.5.cloned.1.call-start = ((), (), s32[]{:S(2)}) async-start(), calls=%async_computation | async-start | bytes 6082560 | tf_op jit(solution)/shard_map/all_gather | solution.py:1049
  10.8 219.7 %all-gather.7.cloned.1.call-start = ((), (), s32[]{:S(2)}) async-start(), calls=%async_computation.1 | async-start | bytes 14598144 | tf_op jit(solution)/shard_map/all_gather | solution.py:1153
  28.9 22.3 %collective-permute-start.3 = (bf16[4,48,1280]{2,1,0:T(8,128)(2,1)}, bf16[4,48,1280]{2,1,0:T(8,128)(2,1)S(1)}, u32[]{:S(2)}, u32[]{:S(2)}) collective-permute-start(bf16[4,48,1280]{2,1,0:T(8,128)(2,1)} %pad_maximum_fusion.1.refs_1_.refs_4_.refs_9_), channel_id=1, source_target_pairs={{0,1},{1,0},{2,3},{3,2},{4,5},{5,4},{6,7},{7,6},{8,9},{9,8},{10,11... | collective-permute-start | bytes 1474568 | tf_op jit(solution)/shard_map/ppermute | solution.py:818
  30.2 23.3 %collective-permute-start.4 = (bf16[4,48,1280]{2,1,0:T(8,128)(2,1)}, bf16[4,48,1280]{2,1,0:T(8,128)(2,1)S(1)}, u32[]{:S(2)}, u32[]{:S(2)}) collective-permute-start(bf16[4,48,1280]{2,1,0:T(8,128)(2,1)} %pad_maximum_fusion.1.refs_1_.refs_4_.refs_9_), channel_id=1, source_target_pairs={{0,16},{8,24},{16,0},{24,8},{1,17},{9,25},{17,1},{25,9},{2,18},{10... | collective-permute-start | bytes 1474568 | tf_op jit(solution)/shard_map/ppermute | solution.py:818
  30.4 25.7 %collective-permute-start.5 = (bf16[4,48,1280]{2,1,0:T(8,128)(2,1)}, bf16[4,48,1280]{2,1,0:T(8,128)(2,1)}, u32[]{:S(2)}, u32[]{:S(2)}) collective-permute-start(bf16[4,48,1280]{2,1,0:T(8,128)(2,1)} %pad_maximum_fusion.1.refs_1_.refs_4_.refs_9_), channel_id=1, source_target_pairs={{0,17},{1,16},{2,19},{3,18},{4,21},{5,20},{6,23},{7,22},{8,25},{9,... | collective-permute-start | bytes 1474568 | tf_op jit(solution)/shard_map/ppermute | solution.py:826
  31.6 14.9 %collective-permute-start.11 = (bf16[48,1536]{1,0:T(8,128)(2,1)}, bf16[48,1536]{1,0:T(8,128)(2,1)}, u32[]{:S(2)}, u32[]{:S(2)}) collective-permute-start(bf16[48,1536]{1,0:T(8,128)(2,1)} %gate.5.refs_1_), channel_id=1, source_target_pairs={{0,4},{1,5},{2,6},{3,7},{4,0},{5,1},{6,2},{7,3},{8,12},{9,13},{10,... | collective-permute-start | bytes 442376 | tf_op jit(solution)/shard_map/ppermute | solution.py:818
  46.4 15.1 %collective-permute-start.6 = (bf16[4,48,1280]{2,1,0:T(8,128)(2,1)}, bf16[4,48,1280]{2,1,0:T(8,128)(2,1)S(1)}, u32[]{:S(2)}, u32[]{:S(2)}) collective-permute-start(bf16[4,48,1280]{2,1,0:T(8,128)(2,1)} %pad_maximum_fusion.1.refs_1_.refs_4_.refs_9_), channel_id=1, source_target_pairs={{0,8},{8,0},{16,24},{24,16},{1,9},{9,1},{17,25},{25,17},{2,10},{10... | collective-permute-start | bytes 1474568 | tf_op jit(solution)/shard_map/ppermute | solution.py:818
  79.7 29.4 %collective-permute-start.16 = (bf16[1024,1536]{1,0:T(8,128)(2,1)}, bf16[1024,1536]{1,0:T(8,128)(2,1)}, u32[]{:S(2)}, u32[]{:S(2)}) collective-permute-start(bf16[1024,1536]{1,0:T(8,128)(2,1)} %get-tuple-element.70.refs_1_.refs_2_.refs_5_), channel_id=1, source_target_pairs={{0,8},{8,0},{16,24},{24,16},{1,9},{9,1},{17,25},{25,17},{2,10},{10... | collective-permute-start | bytes 9437192 | tf_op jit(solution)/shard_map/ppermute | solution.py:818
  79.8 29.3 %collective-permute-start.17 = (bf16[1024,768]{1,0:T(8,128)(2,1)}, bf16[1024,768]{1,0:T(8,128)(2,1)}, u32[]{:S(2)}, u32[]{:S(2)}) collective-permute-start(bf16[1024,768]{1,0:T(8,128)(2,1)} %bitcast.61), channel_id=1, source_target_pairs={{0,8},{8,0},{16,24},{24,16},{1,9},{9,1},{17,25},{25,17},{2,10},{10... | collective-permute-start | bytes 4718600 | tf_op jit(solution)/shard_map/ppermute | solution.py:818
  80.3 28.8 %collective-permute-start.13 = (bf16[4,48,1536]{2,1,0:T(8,128)(2,1)}, bf16[4,48,1536]{2,1,0:T(8,128)(2,1)S(1)}, u32[]{:S(2)}, u32[]{:S(2)}) collective-permute-start(bf16[4,48,1536]{2,1,0:T(8,128)(2,1)} %gate.7.refs_6_.refs_0_), channel_id=1, source_target_pairs={{0,1},{1,0},{2,3},{3,2},{4,5},{5,4},{6,7},{7,6},{8,9},{9,8},{10,11... | collective-permute-start | bytes 1769480 | tf_op jit(solution)/shard_map/ppermute | solution.py:818
  81.6 27.6 %collective-permute-start.14 = (bf16[4,48,1536]{2,1,0:T(8,128)(2,1)}, bf16[4,48,1536]{2,1,0:T(8,128)(2,1)}, u32[]{:S(2)}, u32[]{:S(2)}) collective-permute-start(bf16[4,48,1536]{2,1,0:T(8,128)(2,1)} %gate.7.refs_6_.refs_0_), channel_id=1, source_target_pairs={{0,16},{8,24},{16,0},{24,8},{1,17},{9,25},{17,1},{25,9},{2,18},{10... | collective-permute-start | bytes 1769480 | tf_op jit(solution)/shard_map/ppermute | solution.py:818
  81.8 27.3 %collective-permute-start.15 = (bf16[4,48,1536]{2,1,0:T(8,128)(2,1)}, bf16[4,48,1536]{2,1,0:T(8,128)(2,1)}, u32[]{:S(2)}, u32[]{:S(2)}) collective-permute-start(bf16[4,48,1536]{2,1,0:T(8,128)(2,1)} %gate.7.refs_6_.refs_0_), channel_id=1, source_target_pairs={{0,17},{1,16},{2,19},{3,18},{4,21},{5,20},{6,23},{7,22},{8,25},{9,... | collective-permute-start | bytes 1769480 | tf_op jit(solution)/shard_map/ppermute | solution.py:826
  114.9 25.2 %collective-permute-start.22 = (bf16[1024,3840]{1,0:T(8,128)(2,1)}, bf16[1024,3840]{1,0:T(8,128)(2,1)}, u32[]{:S(2)}, u32[]{:S(2)}) collective-permute-start(bf16[1024,3840]{1,0:T(8,128)(2,1)} %gate.9.refs_14_.refs_1_.refs_2_), channel_id=1, source_target_pairs={{0,8},{8,0},{16,24},{24,16},{1,9},{9,1},{17,25},{25,17},{2,10},{10... | collective-permute-start | bytes 23592968 | tf_op jit(solution)/shard_map/ppermute | solution.py:818
  139.9 15.8 %collective-permute-start.23 = (bf16[1024,2304]{1,0:T(8,128)(2,1)}, bf16[1024,2304]{1,0:T(8,128)(2,1)}, u32[]{:S(2)}, u32[]{:S(2)}) collective-permute-start(bf16[1024,2304]{1,0:T(8,128)(2,1)} %get-tuple-element.84.refs_6_.refs_3_), channel_id=1, source_target_pairs={{0,8},{8,0},{16,24},{24,16},{1,9},{9,1},{17,25},{25,17},{2,10},{10... | collective-permute-start | bytes 14155784 | tf_op jit(solution)/shard_map/ppermute | solution.py:818
  152.1 17.0 %collective-permute-start.25 = (bf16[4,48,1536]{2,1,0:T(8,128)(2,1)}, bf16[4,48,1536]{2,1,0:T(8,128)(2,1)S(1)}, u32[]{:S(2)}, u32[]{:S(2)}) collective-permute-start(bf16[4,48,1536]{2,1,0:T(8,128)(2,1)} %get-tuple-element.90), channel_id=1, source_target_pairs={{0,16},{8,24},{16,0},{24,8},{1,17},{9,25},{17,1},{25,9},{2,18},{10... | collective-permute-start | bytes 1769480 | tf_op jit(solution)/shard_map/ppermute | solution.py:818
  152.4 16.7 %collective-permute-start.26 = (bf16[4,48,1536]{2,1,0:T(8,128)(2,1)}, bf16[4,48,1536]{2,1,0:T(8,128)(2,1)}, u32[]{:S(2)}, u32[]{:S(2)}) collective-permute-start(bf16[4,48,1536]{2,1,0:T(8,128)(2,1)} %get-tuple-element.91), channel_id=1, source_target_pairs={{0,1},{1,0},{2,3},{3,2},{4,5},{5,4},{6,7},{7,6},{8,9},{9,8},{10,11... | collective-permute-start | bytes 1769480 | tf_op jit(solution)/shard_map/ppermute | solution.py:818
  167.6 31.8 %collective-permute-start.27 = (bf16[4,48,1536]{2,1,0:T(8,128)(2,1)}, bf16[4,48,1536]{2,1,0:T(8,128)(2,1)}, u32[]{:S(2)}, u32[]{:S(2)}) collective-permute-start(bf16[4,48,1536]{2,1,0:T(8,128)(2,1)} %get-tuple-element.96), channel_id=1, source_target_pairs={{0,1},{1,0},{2,3},{3,2},{4,5},{5,4},{6,7},{7,6},{8,9},{9,8},{10,11... | collective-permute-start | bytes 1769480 | tf_op jit(solution)/shard_map/ppermute | solution.py:818
  167.9 31.5 %collective-permute-start.28 = (bf16[4,48,1536]{2,1,0:T(8,128)(2,1)}, bf16[4,48,1536]{2,1,0:T(8,128)(2,1)}, u32[]{:S(2)}, u32[]{:S(2)}) collective-permute-start(bf16[4,48,1536]{2,1,0:T(8,128)(2,1)} %get-tuple-element.97), channel_id=1, source_target_pairs={{0,16},{8,24},{16,0},{24,8},{1,17},{9,25},{17,1},{25,9},{2,18},{10... | collective-permute-start | bytes 1769480 | tf_op jit(solution)/shard_map/ppermute | solution.py:818
  187.3 18.8 %collective-permute-start.31 = (bf16[1024,1152]{1,0:T(8,128)(2,1)}, bf16[1024,1152]{1,0:T(8,128)(2,1)}, u32[]{:S(2)}, u32[]{:S(2)}) collective-permute-start(bf16[1024,1152]{1,0:T(8,128)(2,1)} %get-tuple-element.101), channel_id=1, source_target_pairs={{0,8},{8,0},{16,24},{24,16},{1,9},{9,1},{17,25},{25,17},{2,10},{10... | collective-permute-start | bytes 7077896 | tf_op jit(solution)/shard_map/ppermute | solution.py:818
  203.0 18.4 %collective-permute-start.29 = (bf16[2,48,3072]{2,1,0:T(8,128)(2,1)}, bf16[2,48,3072]{2,1,0:T(8,128)(2,1)}, u32[]{:S(2)}, u32[]{:S(2)}) collective-permute-start(bf16[2,48,3072]{2,1,0:T(8,128)(2,1)} %get-tuple-element.98), channel_id=1, source_target_pairs={{0,1},{1,0},{2,3},{3,2},{4,5},{5,4},{6,7},{7,6},{8,9},{9,8},{10,11... | collective-permute-start | bytes 1769480 | tf_op jit(solution)/shard_map/ppermute | solution.py:818
  204.3 17.1 %collective-permute-start.30 = (bf16[2,48,3072]{2,1,0:T(8,128)(2,1)}, bf16[2,48,3072]{2,1,0:T(8,128)(2,1)}, u32[]{:S(2)}, u32[]{:S(2)}) collective-permute-start(bf16[2,48,3072]{2,1,0:T(8,128)(2,1)} %get-tuple-element.99.refs_13_), channel_id=1, source_target_pairs={{0,16},{8,24},{16,0},{24,8},{1,17},{9,25},{17,1},{25,9},{2,18},{10... | collective-permute-start | bytes 1769480 | tf_op jit(solution)/shard_map/ppermute | solution.py:818
  220.4 23.7 %collective-permute-start.33 = (bf16[4,48,1664]{2,1,0:T(8,128)(2,1)}, bf16[4,48,1664]{2,1,0:T(8,128)(2,1)S(1)}, u32[]{:S(2)}, u32[]{:S(2)}) collective-permute-start(bf16[4,48,1664]{2,1,0:T(8,128)(2,1)} %get-tuple-element.106), channel_id=1, source_target_pairs={{0,1},{1,0},{2,3},{3,2},{4,5},{5,4},{6,7},{7,6},{8,9},{9,8},{10,11... | collective-permute-start | bytes 1916936 | tf_op jit(solution)/shard_map/ppermute | solution.py:818
  220.4 23.6 %collective-permute-start.34 = (bf16[4,48,1664]{2,1,0:T(8,128)(2,1)}, bf16[4,48,1664]{2,1,0:T(8,128)(2,1)}, u32[]{:S(2)}, u32[]{:S(2)}) collective-permute-start(bf16[4,48,1664]{2,1,0:T(8,128)(2,1)} %get-tuple-element.107), channel_id=1, source_target_pairs={{0,16},{8,24},{16,0},{24,8},{1,17},{9,25},{17,1},{25,9},{2,18},{10... | collective-permute-start | bytes 1916936 | tf_op jit(solution)/shard_map/ppermute | solution.py:818
  225.4 18.6 %collective-permute-start.35 = (bf16[2,48,3072]{2,1,0:T(8,128)(2,1)}, bf16[2,48,3072]{2,1,0:T(8,128)(2,1)}, u32[]{:S(2)}, u32[]{:S(2)}) collective-permute-start(bf16[2,48,3072]{2,1,0:T(8,128)(2,1)} %get-tuple-element.108), channel_id=1, source_target_pairs={{0,2},{1,3},{2,0},{3,1},{4,6},{5,7},{6,4},{7,5},{8,10},{9,11},{10,... | collective-permute-start | bytes 1769480 | tf_op jit(solution)/shard_map/ppermute | solution.py:818
  (56 other events, 357.8 us)
Sparse Core Ops, SparseCore 0:
  11.6 77.4 all-gather.4
  110.1 120.4 all-gather.6

commit v2 on v1

--- a/solution.py
+++ b/solution.py
@@ -126,8 +126,11 @@
 
     def start(self, refs, place, names, targets, semaphores):
         for name in names:
-            ref = refs[self.asked.index(name)]
-            pltpu.make_async_copy(ref, targets[name], semaphores[name]).start()
+            ref, target = refs[self.asked.index(name)], targets[name]
+            chunks, base, rows = semaphores[name]
+            for chunk in range(target.shape[0] // rows):
+                part = pl.ds(chunk * rows, rows)
+                pltpu.make_async_copy(ref.at[part], target.at[part], chunks.at[base + chunk]).start()
 
 
 def start_piece(source, parts, names, targets, semaphores, f, x, core):
@@ -135,6 +138,8 @@
         part = parts[name]
         height = source.shape[0]
         first = f * (2 * part.folds * height) + x * (part.folds * height)
+        chunks, base, rows = semaphores[name]
+        semaphore = chunks.at[base + lax.div(f * (2 * part.folds * height), rows)]
         for fold in range(part.folds):
             columns = part.start + fold * part.width
             pltpu.make_async_copy(
@@ -143,7 +148,7 @@
                     pl.ds(pl.multiple_of(first + fold * height, 16), height),
                     pl.ds(pl.multiple_of(core * part.width, LANES), part.width),
                 ],
-                semaphores[name],
+                semaphore,
             ).start()
 
 
@@ -196,14 +201,20 @@
         self.arrays = [a for source, names in wanted for a in source.operands(names)]
         self.specs = [pl.BlockSpec(memory_space=pltpu.HBM)] * len(self.arrays)
         self.scratch = [pltpu.VMEM(shapes[name], BF16) for name in self.names] + [
-            pltpu.SemaphoreType.DMA((len(self.names),))
+            pltpu.SemaphoreType.DMA((sum(self.chunks(name) for name in self.names),))
         ]
         self.bytes = sum(2 * shapes[name][0] * shapes[name][1] for name in self.names)
+
+    def chunks(self, name):
+        return self.shapes[name][0] // self.shapes["qkv"][0]
 
     def bind(self, refs, scratch, place_ref):
         self.refs = refs
         self.targets = dict(zip(self.names, scratch))
-        self.semaphores = {name: scratch[-1].at[i] for i, name in enumerate(self.names)}
+        self.semaphores, base = {}, 0
+        for name in self.names:
+            self.semaphores[name] = scratch[-1], base, self.shapes["qkv"][0]
+            base += self.chunks(name)
         self.place = (place_ref[0], place_ref[1], place_ref[2])
         return self
 
@@ -217,9 +228,13 @@
             if names:
                 source.start(refs, self.place, names, self.targets, self.semaphores)
 
-    def wait(self, name):
+    def wait(self, name, only=None):
         target = self.targets[name]
-        pltpu.make_async_copy(target, target, self.semaphores[name]).wait()
+        chunks, base, rows = self.semaphores[name]
+        for chunk in range(self.chunks(name)) if only is None else (only,):
+            start = chunk * rows
+            part = target.at[pl.ds(pl.multiple_of(start, 16), rows)]
+            pltpu.make_async_copy(part, part, chunks.at[base + chunk]).wait()
 
 
 def normed(values, gain, shift):
@@ -378,20 +393,26 @@
         load.start(["fc2"])
         sums_ref[...] = jnp.zeros_like(sums_ref)
         wide_ref[...] = jnp.zeros_like(wide_ref)
-        load.wait("fc2")
         load.start(["fc1", "out"])
 
     g = g_ref[...]
     w_fc2 = load.targets["fc2"]
     step, half = g.shape[1], mine_ref.shape[1]
     starts = [pl.multiple_of(side * half, LANES) for side in (place[2], 1 - place[2])]
-    for start, out in zip(starts, (mine_ref, share_ref)):
-        for at in range(0, half, step):
-            columns = pl.ds(pl.multiple_of(start + at, LANES), step)
-            grad = dot_nt(g, w_fc2[columns, :])
-            low = (grad * slope_ref[:, columns].astype(F32)).astype(BF16)
-            out[:, at : at + step] = low
-            wide_ref[0:1, columns] += jnp.sum(low.astype(F32), axis=0, keepdims=True)
+
+    def steps(arriving):
+        for start, out in zip(starts, (mine_ref, share_ref)):
+            for at in range(0, half, step):
+                if arriving:
+                    load.wait("fc2", lax.div(start + at, step))
+                columns = pl.ds(pl.multiple_of(start + at, LANES), step)
+                grad = dot_nt(g, w_fc2[columns, :])
+                low = (grad * slope_ref[:, columns].astype(F32)).astype(BF16)
+                out[:, at : at + step] = low
+                wide_ref[0:1, columns] += jnp.sum(low.astype(F32), axis=0, keepdims=True)
+
+    pl.when(first)(partial(steps, True))
+    pl.when(jnp.logical_not(first))(partial(steps, False))
 
     @pl.when(first)
     def _():
@@ -1127,7 +1148,6 @@
     )
     done = (pair,)
     if by_pieces:
-        (column_fc2,) = gate([column_fc2], done)
         pieces_fc2 = gather_pieces(column_fc2)
         their_pair, their_cotangent = swap(pair, "dp", 1), swap(cotangent, "dp", 1)
         done = (column_fc2,)

time: 316 us -> 315 us (level)
    pallas_call x22 -> x21, Pallas kernels: 166 us -> 167 us  [call(): pl.pallas_call(ordered, name=name, grid_spec=pltpu.PrefetchScalarGridSpec...]
  transfers between devices with their start and end apart: 47 -> 47, of which waited for: 20 -> 20; matrix products, arithmetic and copies ran while one was open for 5% -> 5% of each run, Pallas kernels for 49% -> 50%
where the time goes in v2:
time: 315 us; the launch traced here: 310 us
  Pallas kernels  167 us (53%)
  waiting for transfers between devices  57.1 us (18%)
  starting transfers between devices  47.7 us (15%)
  local copies, waits for them, and re-layouts  15.9 us (5%)
  between operations  14.9 us (5%)
  other arithmetic  6.98 us (2%)
    pallas_call x21, Pallas kernels, call(): pl.pallas_call(ordered, name=name, grid_spec=pltpu.PrefetchScalarGridSpec...  167 us
    ppermute x43, waiting for transfers between devices, swap(): return lax.ppermute(value, axis, [(i, i ^ bit) for i in range(size)])  48 us
    ppermute x43, starting transfers between devices, swap(): return lax.ppermute(value, axis, [(i, i ^ bit) for i in range(size)])  45.3 us
    unnamed x66, local copies, waits for them, and re-layouts  8.19 us
  transfers between devices with their start and end apart: 47, of which 20 were waited for; matrix products, arithmetic and copies ran while one was open for 5% of the time, Pallas kernels for 50%

profile of v2, /device:TPU:11, one launch (start us, length us, event | category | flops | bytes accessed | tf_op | source)
XLA Modules:
  0.0 309.6 jit_solution(4521114456835609811)
XLA Ops:
  17.3 6.1 %collective-permute-done.2 = bf16[48,1280]{1,0:T(8,128)(2,1)S(1)} collective-permute-done((bf16[48,1280]{1,0:T(8,128)(2,1)}, bf16[48,1280]{1,0:T(8,128)(2,1)S(1)}, u32[]{:S(2)}, u32[]{:S(2)}) %collective-permute-start.2) | collective-permute-done | bytes 122912 | tf_op jit(solution)/shard_map/ppermute | solution.py:839
  23.4 3.3 %collective-permute-done.1 = bf16[48,1280]{1,0:T(8,128)(2,1)S(1)} collective-permute-done((bf16[48,1280]{1,0:T(8,128)(2,1)}, bf16[48,1280]{1,0:T(8,128)(2,1)S(1)}, u32[]{:S(2)}, u32[]{:S(2)}) %collective-permute-start.1) | collective-permute-done | bytes 122912 | tf_op jit(solution)/shard_map/ppermute | solution.py:839
  31.5 3.8 %collective-permute-start.11 = (bf16[48,1536]{1,0:T(8,128)(2,1)}, bf16[48,1536]{1,0:T(8,128)(2,1)}, u32[]{:S(2)}, u32[]{:S(2)}) collective-permute-start(bf16[48,1536]{1,0:T(8,128)(2,1)} %gate.4.refs_1_), channel_id=1, source_target_pairs={{0,4},{1,5},{2,6},{3,7},{4,0},{5,1},{6,2},{7,3},{8,12},{9,13},{10,... | collective-permute-start | bytes 442376 | tf_op jit(solution)/shard_map/ppermute | solution.py:839
  41.3 4.8 %collective-permute-done.11 = bf16[48,1536]{1,0:T(8,128)(2,1)} collective-permute-done((bf16[48,1536]{1,0:T(8,128)(2,1)}, bf16[48,1536]{1,0:T(8,128)(2,1)}, u32[]{:S(2)}, u32[]{:S(2)}) %collective-permute-start.11) | collective-permute-done | bytes 147488 | tf_op jit(solution)/shard_map/ppermute | solution.py:839
  56.1 3.7 %collective-permute-start.9 = (bf16[4,48,1280]{2,1,0:T(8,128)(2,1)}, bf16[4,48,1280]{2,1,0:T(8,128)(2,1)S(1)}, u32[]{:S(2)}, u32[]{:S(2)}) collective-permute-start(bf16[4,48,1280]{2,1,0:T(8,128)(2,1)} %collective-permute-done.5.refs_7_.refs_12_), channel_id=1, source_target_pairs={{0,8},{8,0},{16,24},{24,16},{1,9},{9,1},{17,25},{25,17},{2,10},{10... | collective-permute-start | bytes 1474568 | tf_op jit(solution)/shard_map/ppermute | solution.py:839
  63.5 15.8 %text_attend.1 = (bf16[1024,1536]{1,0:T(8,128)(2,1)}, bf16[1024,2304]{1,0:T(8,128)(2,1)}, bf16[8,6,128,256]{3,2,1,0:T(8,128)(2,1)}, f32[1024,768]{1,0:T(8,128)}) custom-call(s32[3]{0:T(128)} %pad_add_fusion.refs_0_, bf16[1024,768]{1,0:T(8,128)(2,1)} %bitcast.65, f32[8,1,128]{2,1,0:T(1,128)} %reshape.72.refs_2_, ...), custom_call_target="tpu_custom_call" | custom-call | flops 4831838208 | bytes 22413312 | tf_op jit(solution)/shard_map/text_attend/pallas_call | solution.py:45
  83.3 5.5 %all-gather.5.cloned.1.call-done = bf16[1536,1920]{1,0:T(8,128)(2,1)} async-done(((bf16[48,1920]{1,0:T(8,128)(2,1)}), bf16[1536,1920]{1,0:T(8,128)(2,1)}) %all-gather.5.cloned.1.call-update) | async-done | bytes 5898256 | tf_op jit(solution)/shard_map/all_gather | solution.py:1070
  88.8 19.9 %text_forward.1 = (f32[1024,768]{1,0:T(8,128)}, bf16[1024,3840]{1,0:T(8,128)(2,1)}, bf16[1024,3072]{1,0:T(8,128)(2,1)}) custom-call(s32[3]{0:T(128)} %pad_add_fusion.refs_0_, bf16[1024,768]{1,0:T(8,128)(2,1)} %bitcast.66, bf16[1024,1536]{1,0:T(8,128)(2,1)} %get-tuple-element.70.refs_2_.refs_1_.refs_5_, ...), custom_call_target="tpu_custom_call" | custom-call | flops 6039797760 | bytes 26345472 | tf_op jit(solution)/shard_map/text_forward/pallas_call | solution.py:45
  114.6 24.0 %text_back.1 = (bf16[1024,1536]{1,0:T(8,128)(2,1)}, bf16[1024,2304]{1,0:T(8,128)(2,1)}, bf16[1024,768]{1,0:T(8,128)(2,1)}, f32[8,768]{1,0:T(8,128)}, f32[8,3072]{1,0:T(8,128)}) custom-call(s32[3]{0:T(128)} %pad_add_fusion.refs_0_, bf16[1024,768]{1,0:T(8,128)(2,1)} %bitcast.62, f32[1024,768]{1,0:T(8,128)} %get-tuple-element.72.refs_2_.refs_1_, ...), custom_call_target="tpu_custom_call" | custom-call | flops 10871635968 | bytes 35782656 | tf_op jit(solution)/shard_map/text_back/pallas_call | solution.py:45
  138.7 12.1 %grads_one.1 = (bf16[4,48,1536]{2,1,0:T(8,128)(2,1)}, bf16[4,48,1536]{2,1,0:T(8,128)(2,1)}, bf16[4,48,1536]{2,1,0:T(8,128)(2,1)}, bf16[4,48,1536]{2,1,0:T(8,128)(2,1)}) custom-call(s32[3]{0:T(128)} %pad_add_fusion.refs_0_, bf16[1024,3840]{1,0:T(8,128)(2,1)} %gate.7.refs_14_.refs_1_.refs_2_, bf16[1024,3840]{1,0:T(8,128)(2,1)} %collective-permute-done.22.refs_2_, ...), custom_call_target="tpu_custom_call" | custom-call | flops 4831838208 | bytes 18874368 | tf_op jit(solution)/shard_map/grads_one/pallas_call | solution.py:45
  154.6 11.8 %grads_two.1 = (bf16[4,48,1536]{2,1,0:T(8,128)(2,1)}, bf16[4,48,1536]{2,1,0:T(8,128)(2,1)}, bf16[4,48,1536]{2,1,0:T(8,128)(2,1)}, bf16[4,48,1536]{2,1,0:T(8,128)(2,1)}) custom-call(s32[3]{0:T(128)} %pad_add_fusion.refs_0_, bf16[1024,3840]{1,0:T(8,128)(2,1)} %gate.7.refs_14_.refs_1_.refs_2_, bf16[1024,3840]{1,0:T(8,128)(2,1)} %collective-permute-done.22.refs_2_, ...), custom_call_target="tpu_custom_call" | custom-call | flops 4831838208 | bytes 23592960 | tf_op jit(solution)/shard_map/grads_two/pallas_call | solution.py:45
  168.8 18.3 %text_unjoin.1 = (bf16[1024,2304]{1,0:T(8,128)(2,1)}, bf16[1024,1152]{1,0:T(8,128)(2,1)}, f32[1024,768]{1,0:T(8,128)}, f32[8,768]{1,0:T(8,128)}) custom-call(s32[3]{0:T(128)} %pad_add_fusion.refs_0_, bf16[1024,2304]{1,0:T(8,128)(2,1)} %get-tuple-element.79.refs_1_, bf16[8,6,128,256]{3,2,1,0:T(8,128)(2,1)} %get-tuple-element.80.refs_2_, ...), custom_call_target="tpu_custom_call" | custom-call | flops 6039797760 | bytes 28704768 | tf_op jit(solution)/shard_map/text_unjoin/pallas_call | solution.py:45
  187.5 11.7 %text_out.1.refs_9_ = bf16[1024,768]{1,0:T(8,128)(2,1)} custom-call(s32[3]{0:T(128)} %pad_add_fusion.refs_0_, f32[1024,768]{1,0:T(8,128)} %get-tuple-element.72.refs_2_.refs_1_, bf16[1024,3840]{1,0:T(8,128)(2,1)} %gate.7.refs_14_.refs_1_.refs_2_, f32[16,768]{1,0:T(8,128)} %convert_element_type.19.refs_3_.refs_4_.refs_7_.refs_2_, ...), custom_call_target="tpu_custom_call" | custom-call | flops 4831838208 | bytes 15728640 | tf_op jit(solution)/shard_map/text_out/pallas_call | solution.py:45
  199.2 3.7 %sums_one.1 = (bf16[2,48,3072]{2,1,0:T(8,128)(2,1)}, bf16[2,48,3072]{2,1,0:T(8,128)(2,1)}) custom-call(s32[3]{0:T(128)} %pad_add_fusion.refs_0_, bf16[4,48,1536]{2,1,0:T(8,128)(2,1)} %get-tuple-element.94.refs_1_.refs_5_, bf16[4,48,1536]{2,1,0:T(8,128)(2,1)} %collective-permute-done.26.refs_20_.refs_2_.refs_8_, ...), custom_call_target="tpu_custom_call" | custom-call | flops 58982400000 | bytes 4718592 | tf_op jit(solution)/shard_map/sums_one/pallas_call | solution.py:45
  206.6 13.4 %grads_three.1 = (bf16[4,48,1664]{2,1,0:T(8,128)(2,1)}, bf16[4,48,1664]{2,1,0:T(8,128)(2,1)}, bf16[4,48,1664]{2,1,0:T(8,128)(2,1)}, bf16[4,48,1664]{2,1,0:T(8,128)(2,1)}) custom-call(s32[3]{0:T(128)} %pad_add_fusion.refs_0_, bf16[1024,1536]{1,0:T(8,128)(2,1)} %get-tuple-element.70.refs_2_.refs_1_.refs_5_, ...), custom_call_target="tpu_custom_call" | custom-call | flops 4831838208 | bytes 29147136 | tf_op jit(solution)/shard_map/grads_three/pallas_call | solution.py:45
  221.7 4.2 %sums_two.1 = (bf16[2,48,3072]{2,1,0:T(8,128)(2,1)}, bf16[2,48,3072]{2,1,0:T(8,128)(2,1)}) custom-call(s32[3]{0:T(128)} %pad_add_fusion.refs_0_, bf16[4,48,1536]{2,1,0:T(8,128)(2,1)} %get-tuple-element.87.refs_5_.refs_1_.refs_7_, bf16[4,48,1536]{2,1,0:T(8,128)(2,1)} %copy-done.4, bf16[2,48,3072]{2,1,0:T(8,128)(2,1)} %collective-permute-done.29.refs_3_.refs_6_, ...), custom_call_target="tpu_custom_call" | custom-call | flops 589824 | bytes 4718592 | tf_op jit(solution)/shard_map/sums_two/pallas_call | solution.py:45
  229.5 13.5 %image_block.1.refs_9_ = bf16[4,50,768]{2,1,0:T(8,128)(2,1)} custom-call(s32[3]{0:T(128)} %pad_add_fusion.refs_0_, bf16[4,50,768]{2,1,0:T(8,128)(2,1)} %gate.5.refs_13_.refs_1_, f32[16,768]{1,0:T(8,128)} %convert_element_type.19.refs_3_.refs_4_.refs_7_.refs_2_, bf16[32,48,4608]{2,1,0:T(8,128)(2,1)} %bitcast.55, ...), custom_call_target="tpu_custom_call" | custom-call | flops 3623878656 | bytes 14942208 | tf_op jit(solution)/shard_map/image_block/pallas_call | solution.py:45
  243.8 3.2 %sums_three.1 = (bf16[2,48,1664]{2,1,0:T(8,128)(2,1)}, bf16[2,48,1664]{2,1,0:T(8,128)(2,1)}, bf16[1,48,3072]{2,1,0:T(8,128)(2,1)}, bf16[1,48,3072]{2,1,0:T(8,128)(2,1)}) custom-call(s32[3]{0:T(128)} %pad_add_fusion.refs_0_, bf16[4,48,1664]{2,1,0:T(8,128)(2,1)} %get-tuple-element.105.refs_1_.refs_3_, bf16[4,48,1664]{2,1,0:T(8,128)(2,1)} %copy-done, ...), custom_call_target="tpu_custom_call" | custom-call | flops 614400 | bytes 4915200 | tf_op jit(solution)/shard_map/sums_three/pallas_call | solution.py:45
  250.1 6.3 %collective-permute-done.37.refs_3_.refs_6_ = bf16[2,48,1664]{2,1,0:T(8,128)(2,1)S(1)} collective-permute-done((bf16[2,48,1664]{2,1,0:T(8,128)(2,1)}, bf16[2,48,1664]{2,1,0:T(8,128)(2,1)S(1)}, u32[]{:S(2)}, u32[]{:S(2)}) %collective-permute-start.37) | collective-permute-done | bytes 319520 | tf_op jit(solution)/shard_map/ppermute | solution.py:839
  258.5 3.3 %sums_four.1 = (bf16[1,48,1664]{2,1,0:T(8,128)(2,1)}, bf16[1,48,1664]{2,1,0:T(8,128)(2,1)}, bf16[1,48,1664]{2,1,0:T(8,128)(2,1)}, bf16[1,48,1664]{2,1,0:T(8,128)(2,1)}) custom-call(s32[3]{0:T(128)} %pad_add_fusion.refs_0_, bf16[4,48,1664]{2,1,0:T(8,128)(2,1)} %get-tuple-element.103.refs_13_.refs_1_.refs_4_.refs_7_.refs_10_, ...), custom_call_target="tpu_custom_call" | custom-call | flops 319488 | bytes 2555904 | tf_op jit(solution)/shard_map/sums_four/pallas_call | solution.py:45
  264.5 5.8 %collective-permute-done.39.refs_4_ = bf16[1,48,1664]{2,1,0:T(8,128)(2,1)S(1)} collective-permute-done((bf16[1,48,1664]{2,1,0:T(8,128)(2,1)}, bf16[1,48,1664]{2,1,0:T(8,128)(2,1)S(1)}, u32[]{:S(2)}, u32[]{:S(2)}) %collective-permute-start.39) | collective-permute-done | bytes 159776 | tf_op jit(solution)/shard_map/ppermute | solution.py:839
  270.8 7.2 %collective-permute-done.41.refs_6_ = bf16[1,48,1664]{2,1,0:T(8,128)(2,1)S(1)} collective-permute-done((bf16[1,48,1664]{2,1,0:T(8,128)(2,1)}, bf16[1,48,1664]{2,1,0:T(8,128)(2,1)S(1)}, u32[]{:S(2)}, u32[]{:S(2)}) %collective-permute-start.41) | collective-permute-done | bytes 159776 | tf_op jit(solution)/shard_map/ppermute | solution.py:839
  285.3 6.4 %collective-permute-done.42.refs_2_ = bf16[48,4736]{1,0:T(8,128)(2,1)S(1)} collective-permute-done((bf16[48,4736]{1,0:T(8,128)(2,1)}, bf16[48,4736]{1,0:T(8,128)(2,1)S(1)}, u32[]{:S(2)}, u32[]{:S(2)}) %collective-permute-start.42) | collective-permute-done | bytes 454688 | tf_op jit(solution)/shard_map/ppermute | solution.py:839
  296.2 4.1 %finish.1 = (f32[384,768]{1,0:T(8,128)}, f32[96,3072]{1,0:T(8,128)}, f32[96,768]{1,0:T(8,128)}, f32[96,2304]{1,0:T(8,128)}, f32[96,256]{1,0:T(8,128)}) custom-call(s32[3]{0:T(128)} %pad_add_fusion.refs_0_, bf16[48,4736]{1,0:T(8,128)(2,1)} %bitcast.60, bf16[48,4736]{1,0:T(8,128)(2,1)} %copy-done.13, bf16[48,4736]{1,0:T(8,128)(2,1)} %collective-permute-done.43.refs_3_, ...), custom_call_target="tpu_custom_call" | custom-call | bytes 5455872 | tf_op jit(solution)/shard_map/finish/pallas_call | solution.py:45
  (195 shorter events, 82.8 us)
Async XLA Ops:
  7.3 81.5 %all-gather.5.cloned.1.call-start = ((), (), s32[]{:S(2)}) async-start(), calls=%async_computation | async-start | bytes 6082560 | tf_op jit(solution)/shard_map/all_gather | solution.py:1070
  10.7 218.7 %all-gather.7.cloned.1.call-start = ((), (), s32[]{:S(2)}) async-start(), calls=%async_computation.1 | async-start | bytes 14598144 | tf_op jit(solution)/shard_map/all_gather | solution.py:1173
  28.8 22.3 %collective-permute-start.3 = (bf16[4,48,1280]{2,1,0:T(8,128)(2,1)}, bf16[4,48,1280]{2,1,0:T(8,128)(2,1)S(1)}, u32[]{:S(2)}, u32[]{:S(2)}) collective-permute-start(bf16[4,48,1280]{2,1,0:T(8,128)(2,1)} %pad_maximum_fusion.1.refs_1_.refs_4_.refs_9_), channel_id=1, source_target_pairs={{0,1},{1,0},{2,3},{3,2},{4,5},{5,4},{6,7},{7,6},{8,9},{9,8},{10,11... | collective-permute-start | bytes 1474568 | tf_op jit(solution)/shard_map/ppermute | solution.py:839
  30.1 23.3 %collective-permute-start.4 = (bf16[4,48,1280]{2,1,0:T(8,128)(2,1)}, bf16[4,48,1280]{2,1,0:T(8,128)(2,1)S(1)}, u32[]{:S(2)}, u32[]{:S(2)}) collective-permute-start(bf16[4,48,1280]{2,1,0:T(8,128)(2,1)} %pad_maximum_fusion.1.refs_1_.refs_4_.refs_9_), channel_id=1, source_target_pairs={{0,16},{8,24},{16,0},{24,8},{1,17},{9,25},{17,1},{25,9},{2,18},{10... | collective-permute-start | bytes 1474568 | tf_op jit(solution)/shard_map/ppermute | solution.py:839
  30.4 25.7 %collective-permute-start.5 = (bf16[4,48,1280]{2,1,0:T(8,128)(2,1)}, bf16[4,48,1280]{2,1,0:T(8,128)(2,1)}, u32[]{:S(2)}, u32[]{:S(2)}) collective-permute-start(bf16[4,48,1280]{2,1,0:T(8,128)(2,1)} %pad_maximum_fusion.1.refs_1_.refs_4_.refs_9_), channel_id=1, source_target_pairs={{0,17},{1,16},{2,19},{3,18},{4,21},{5,20},{6,23},{7,22},{8,25},{9,... | collective-permute-start | bytes 1474568 | tf_op jit(solution)/shard_map/ppermute | solution.py:847
  31.5 14.6 %collective-permute-start.11 = (bf16[48,1536]{1,0:T(8,128)(2,1)}, bf16[48,1536]{1,0:T(8,128)(2,1)}, u32[]{:S(2)}, u32[]{:S(2)}) collective-permute-start(bf16[48,1536]{1,0:T(8,128)(2,1)} %gate.4.refs_1_), channel_id=1, source_target_pairs={{0,4},{1,5},{2,6},{3,7},{4,0},{5,1},{6,2},{7,3},{8,12},{9,13},{10,... | collective-permute-start | bytes 442376 | tf_op jit(solution)/shard_map/ppermute | solution.py:839
  46.1 15.4 %collective-permute-start.6 = (bf16[4,48,1280]{2,1,0:T(8,128)(2,1)}, bf16[4,48,1280]{2,1,0:T(8,128)(2,1)S(1)}, u32[]{:S(2)}, u32[]{:S(2)}) collective-permute-start(bf16[4,48,1280]{2,1,0:T(8,128)(2,1)} %pad_maximum_fusion.1.refs_1_.refs_4_.refs_9_), channel_id=1, source_target_pairs={{0,8},{8,0},{16,24},{24,16},{1,9},{9,1},{17,25},{25,17},{2,10},{10... | collective-permute-start | bytes 1474568 | tf_op jit(solution)/shard_map/ppermute | solution.py:839
  79.4 29.4 %collective-permute-start.16 = (bf16[1024,1536]{1,0:T(8,128)(2,1)}, bf16[1024,1536]{1,0:T(8,128)(2,1)}, u32[]{:S(2)}, u32[]{:S(2)}) collective-permute-start(bf16[1024,1536]{1,0:T(8,128)(2,1)} %get-tuple-element.70.refs_2_.refs_1_.refs_5_), channel_id=1, source_target_pairs={{0,8},{8,0},{16,24},{24,16},{1,9},{9,1},{17,25},{25,17},{2,10},{10... | collective-permute-start | bytes 9437192 | tf_op jit(solution)/shard_map/ppermute | solution.py:839
  79.4 29.3 %collective-permute-start.17 = (bf16[1024,768]{1,0:T(8,128)(2,1)}, bf16[1024,768]{1,0:T(8,128)(2,1)}, u32[]{:S(2)}, u32[]{:S(2)}) collective-permute-start(bf16[1024,768]{1,0:T(8,128)(2,1)} %bitcast.61), channel_id=1, source_target_pairs={{0,8},{8,0},{16,24},{24,16},{1,9},{9,1},{17,25},{25,17},{2,10},{10... | collective-permute-start | bytes 4718600 | tf_op jit(solution)/shard_map/ppermute | solution.py:839
  79.9 28.8 %collective-permute-start.13 = (bf16[4,48,1536]{2,1,0:T(8,128)(2,1)S(1)}, bf16[4,48,1536]{2,1,0:T(8,128)(2,1)}, u32[]{:S(2)}, u32[]{:S(2)}) collective-permute-start(bf16[4,48,1536]{2,1,0:T(8,128)(2,1)S(1)} %copy-done.1), channel_id=1, source_target_pairs={{0,1},{1,0},{2,3},{3,2},{4,5},{5,4},{6,7},{7,6},{8,9},{9,8},{10,11... | collective-permute-start | bytes 1769480 | tf_op jit(solution)/shard_map/ppermute | solution.py:839
  81.2 27.6 %collective-permute-start.14 = (bf16[4,48,1536]{2,1,0:T(8,128)(2,1)S(1)}, bf16[4,48,1536]{2,1,0:T(8,128)(2,1)}, u32[]{:S(2)}, u32[]{:S(2)}) collective-permute-start(bf16[4,48,1536]{2,1,0:T(8,128)(2,1)S(1)} %copy-done.1), channel_id=1, source_target_pairs={{0,16},{8,24},{16,0},{24,8},{1,17},{9,25},{17,1},{25,9},{2,18},{10... | collective-permute-start | bytes 1769480 | tf_op jit(solution)/shard_map/ppermute | solution.py:839
  81.5 27.3 %collective-permute-start.15 = (bf16[4,48,1536]{2,1,0:T(8,128)(2,1)S(1)}, bf16[4,48,1536]{2,1,0:T(8,128)(2,1)}, u32[]{:S(2)}, u32[]{:S(2)}) collective-permute-start(bf16[4,48,1536]{2,1,0:T(8,128)(2,1)S(1)} %copy-done.1), channel_id=1, source_target_pairs={{0,17},{1,16},{2,19},{3,18},{4,21},{5,20},{6,23},{7,22},{8,25},{9,... | collective-permute-start | bytes 1769480 | tf_op jit(solution)/shard_map/ppermute | solution.py:847
  114.2 24.5 %collective-permute-start.22 = (bf16[1024,3840]{1,0:T(8,128)(2,1)}, bf16[1024,3840]{1,0:T(8,128)(2,1)}, u32[]{:S(2)}, u32[]{:S(2)}) collective-permute-start(bf16[1024,3840]{1,0:T(8,128)(2,1)} %gate.7.refs_14_.refs_1_.refs_2_), channel_id=1, source_target_pairs={{0,8},{8,0},{16,24},{24,16},{1,9},{9,1},{17,25},{25,17},{2,10},{10... | collective-permute-start | bytes 23592968 | tf_op jit(solution)/shard_map/ppermute | solution.py:839
  138.6 16.0 %collective-permute-start.23 = (bf16[1024,2304]{1,0:T(8,128)(2,1)}, bf16[1024,2304]{1,0:T(8,128)(2,1)}, u32[]{:S(2)}, u32[]{:S(2)}) collective-permute-start(bf16[1024,2304]{1,0:T(8,128)(2,1)} %get-tuple-element.84.refs_6_.refs_3_), channel_id=1, source_target_pairs={{0,8},{8,0},{16,24},{24,16},{1,9},{9,1},{17,25},{25,17},{2,10},{10... | collective-permute-start | bytes 14155784 | tf_op jit(solution)/shard_map/ppermute | solution.py:839
  150.8 17.2 %collective-permute-start.25 = (bf16[4,48,1536]{2,1,0:T(8,128)(2,1)}, bf16[4,48,1536]{2,1,0:T(8,128)(2,1)S(1)}, u32[]{:S(2)}, u32[]{:S(2)}) collective-permute-start(bf16[4,48,1536]{2,1,0:T(8,128)(2,1)} %get-tuple-element.90), channel_id=1, source_target_pairs={{0,16},{8,24},{16,0},{24,8},{1,17},{9,25},{17,1},{25,9},{2,18},{10... | collective-permute-start | bytes 1769480 | tf_op jit(solution)/shard_map/ppermute | solution.py:839
  151.1 16.9 %collective-permute-start.26 = (bf16[4,48,1536]{2,1,0:T(8,128)(2,1)}, bf16[4,48,1536]{2,1,0:T(8,128)(2,1)}, u32[]{:S(2)}, u32[]{:S(2)}) collective-permute-start(bf16[4,48,1536]{2,1,0:T(8,128)(2,1)} %get-tuple-element.91), channel_id=1, source_target_pairs={{0,1},{1,0},{2,3},{3,2},{4,5},{5,4},{6,7},{7,6},{8,9},{9,8},{10,11... | collective-permute-start | bytes 1769480 | tf_op jit(solution)/shard_map/ppermute | solution.py:839
  166.4 32.7 %collective-permute-start.27 = (bf16[4,48,1536]{2,1,0:T(8,128)(2,1)}, bf16[4,48,1536]{2,1,0:T(8,128)(2,1)}, u32[]{:S(2)}, u32[]{:S(2)}) collective-permute-start(bf16[4,48,1536]{2,1,0:T(8,128)(2,1)} %get-tuple-element.96), channel_id=1, source_target_pairs={{0,1},{1,0},{2,3},{3,2},{4,5},{5,4},{6,7},{7,6},{8,9},{9,8},{10,11... | collective-permute-start | bytes 1769480 | tf_op jit(solution)/shard_map/ppermute | solution.py:839
  166.8 32.4 %collective-permute-start.28 = (bf16[4,48,1536]{2,1,0:T(8,128)(2,1)}, bf16[4,48,1536]{2,1,0:T(8,128)(2,1)}, u32[]{:S(2)}, u32[]{:S(2)}) collective-permute-start(bf16[4,48,1536]{2,1,0:T(8,128)(2,1)} %get-tuple-element.97), channel_id=1, source_target_pairs={{0,16},{8,24},{16,0},{24,8},{1,17},{9,25},{17,1},{25,9},{2,18},{10... | collective-permute-start | bytes 1769480 | tf_op jit(solution)/shard_map/ppermute | solution.py:839
  187.2 18.8 %collective-permute-start.31 = (bf16[1024,1152]{1,0:T(8,128)(2,1)}, bf16[1024,1152]{1,0:T(8,128)(2,1)}, u32[]{:S(2)}, u32[]{:S(2)}) collective-permute-start(bf16[1024,1152]{1,0:T(8,128)(2,1)} %get-tuple-element.101), channel_id=1, source_target_pairs={{0,8},{8,0},{16,24},{24,16},{1,9},{9,1},{17,25},{25,17},{2,10},{10... | collective-permute-start | bytes 7077896 | tf_op jit(solution)/shard_map/ppermute | solution.py:839
  202.9 18.9 %collective-permute-start.29 = (bf16[2,48,3072]{2,1,0:T(8,128)(2,1)}, bf16[2,48,3072]{2,1,0:T(8,128)(2,1)}, u32[]{:S(2)}, u32[]{:S(2)}) collective-permute-start(bf16[2,48,3072]{2,1,0:T(8,128)(2,1)} %get-tuple-element.98), channel_id=1, source_target_pairs={{0,1},{1,0},{2,3},{3,2},{4,5},{5,4},{6,7},{7,6},{8,9},{9,8},{10,11... | collective-permute-start | bytes 1769480 | tf_op jit(solution)/shard_map/ppermute | solution.py:839
  204.1 17.6 %collective-permute-start.30 = (bf16[2,48,3072]{2,1,0:T(8,128)(2,1)}, bf16[2,48,3072]{2,1,0:T(8,128)(2,1)}, u32[]{:S(2)}, u32[]{:S(2)}) collective-permute-start(bf16[2,48,3072]{2,1,0:T(8,128)(2,1)} %get-tuple-element.99.refs_13_), channel_id=1, source_target_pairs={{0,16},{8,24},{16,0},{24,8},{1,17},{9,25},{17,1},{25,9},{2,18},{10... | collective-permute-start | bytes 1769480 | tf_op jit(solution)/shard_map/ppermute | solution.py:839
  220.0 22.9 %collective-permute-start.33 = (bf16[4,48,1664]{2,1,0:T(8,128)(2,1)}, bf16[4,48,1664]{2,1,0:T(8,128)(2,1)S(1)}, u32[]{:S(2)}, u32[]{:S(2)}) collective-permute-start(bf16[4,48,1664]{2,1,0:T(8,128)(2,1)} %get-tuple-element.106), channel_id=1, source_target_pairs={{0,1},{1,0},{2,3},{3,2},{4,5},{5,4},{6,7},{7,6},{8,9},{9,8},{10,11... | collective-permute-start | bytes 1916936 | tf_op jit(solution)/shard_map/ppermute | solution.py:839
  220.6 22.4 %collective-permute-start.34 = (bf16[4,48,1664]{2,1,0:T(8,128)(2,1)}, bf16[4,48,1664]{2,1,0:T(8,128)(2,1)}, u32[]{:S(2)}, u32[]{:S(2)}) collective-permute-start(bf16[4,48,1664]{2,1,0:T(8,128)(2,1)} %get-tuple-element.107), channel_id=1, source_target_pairs={{0,16},{8,24},{16,0},{24,8},{1,17},{9,25},{17,1},{25,9},{2,18},{10... | collective-permute-start | bytes 1916936 | tf_op jit(solution)/shard_map/ppermute | solution.py:839
  226.0 17.0 %collective-permute-start.35 = (bf16[2,48,3072]{2,1,0:T(8,128)(2,1)}, bf16[2,48,3072]{2,1,0:T(8,128)(2,1)}, u32[]{:S(2)}, u32[]{:S(2)}) collective-permute-start(bf16[2,48,3072]{2,1,0:T(8,128)(2,1)} %get-tuple-element.108), channel_id=1, source_target_pairs={{0,2},{1,3},{2,0},{3,1},{4,6},{5,7},{6,4},{7,5},{8,10},{9,11},{10,... | collective-permute-start | bytes 1769480 | tf_op jit(solution)/shard_map/ppermute | solution.py:839
  (56 other events, 383.1 us)
Sparse Core Ops, SparseCore 0:
  11.6 77.1 all-gather.4
  109.0 120.4 all-gather.6
